TPU v7x, 32 devices: a whole 2x2x4 slice. The times are simulated.
32 devices in a mesh: dp: 4 (over z), ctx: 8 (over y, x, core).
Axes of the slice: x: 2, y: 2, z: 4, core: 2. Of those that a mesh axis runs over, the one named last changes fastest.
Arguments:
- tokens: bfloat16 [8, 1024, 768], P('dp', 'ctx'), may hold values from -6 to 6
- attn_qkv: bfloat16 [3, 768, 768], P(None, ('dp', 'ctx')), may hold values from -0.21875 to 0.21875
- attn_out: bfloat16 [768, 768], P(('dp', 'ctx')), may hold values from -1.75 to 1.75
- norm_gains: bfloat16 [2, 768], P(None, ('dp', 'ctx')), may hold values from 0.5 to 1.5
- router: bfloat16 [768, 8], P(('dp', 'ctx')), may hold values from -0.109375 to 0.109375
- rel_table: bfloat16 [384], P(('dp', 'ctx')), may hold values from -4 to 4
- w_in: bfloat16 [8, 768, 3072], P('ctx', 'dp'), may hold values from -0.21875 to 0.21875
- w_out: bfloat16 [8, 3072, 768], P('ctx', 'dp'), may hold values from -3.5 to 3.5
- cotangent: bfloat16 [8, 1024, 768], P('dp', 'ctx'), may hold values from -6 to 6
- segments: int32 [8, 1024], P('dp', 'ctx'), may hold values from -1 to 4, as said below
- buckets: int32 [2047], replicated, may hold values from 0 to 31
- expert_ids: int32 [8, 1024], P('dp', 'ctx'), may hold values from 0 to 7, as said below
- slots: int32 [8, 1024], P('dp', 'ctx'), may hold values from 0 to 28, as said below
Outputs:
- output: bfloat16 [8, 1024, 768], P('dp', 'ctx')
- grad_tokens: float32 [8, 1024, 768], P('dp', 'ctx')
- grad_attn_qkv: float32 [3, 768, 768], P(None, ('dp', 'ctx'))
- grad_attn_out: float32 [768, 768], P(('dp', 'ctx'))
- grad_norm_gains: float32 [2, 768], P(None, ('dp', 'ctx'))
- grad_router: float32 [768, 8], P(('dp', 'ctx'))
- grad_rel_table: float32 [384], P(('dp', 'ctx'))
- grad_w_in: float32 [8, 768, 3072], P('ctx', 'dp')
- grad_w_out: float32 [8, 3072, 768], P('ctx', 'dp')
Inputs may be any that keep to these rules, and one draw needn't show every extreme that they name: `segments`: along each sequence the document numbers start at 0 and never fall up to the padding. Of the 2 sequences from each multiple of 2, one is a single document with no padding, each of the others holds five documents, and exactly one of those others ends in 256 padding positions numbered -1. `expert_ids`: A capacity group is the positions of the 1 sequence from a multiple of 1, within one block of 128 positions from a multiple of 128. In a group no two positions share both expert id and slot; padding positions carry ids and slots too. In each capacity group one expert holds slots 0 to 28, the same expert in all groups of the same sequences; the other experts hold slots under 21.
All inputs are finite; a program needn't handle non-finite values.
Results may differ from a plain program's by a relative error of at most 0.02.
Values may be sent and summed in bfloat16 or wider, within the bound.
A program may use at most 192 MiB of HBM per device.

v0:
```python
import jax
import jax.numpy as jnp
from jax import lax
from jax.sharding import PartitionSpec as P

H = 12
DH = 64
FF = 3072
NB = 32
SEQ_MB = 1
MICRO = 2


epsilon = 1e-06
precise = lax.Precision.HIGHEST
masked_score = -1000000000.0


def rms_scale(values, gain_row):
    return (
        values * lax.rsqrt(jnp.mean(values * values, axis=-1, keepdims=True) + epsilon) * gain_row
    )


def gelu_tanh(values):
    return jax.nn.gelu(values, approximate=True)


def gather_layer(attn_qkv, attn_out, norm_gains, router, rel_table):
    return (
        lax.all_gather(attn_qkv, ("dp", "ctx"), axis=1, tiled=True),
        lax.all_gather(attn_out, ("dp", "ctx"), axis=0, tiled=True),
        lax.all_gather(norm_gains, ("dp", "ctx"), axis=1, tiled=True),
        lax.all_gather(router, ("dp", "ctx"), axis=0, tiled=True),
        lax.all_gather(rel_table, ("dp", "ctx"), axis=0, tiled=True),
    )


def gather_experts(w_in, w_out):
    return (
        lax.all_gather(w_in, "dp", axis=1, tiled=True),
        lax.all_gather(w_out, "dp", axis=1, tiled=True),
    )


def bias_block(buckets, table_low, query_start, query_count, key_count, length):
    query_pos = query_start + jnp.arange(query_count, dtype=jnp.int32)
    key_pos = jnp.arange(key_count, dtype=jnp.int32)
    bucket_ids = buckets[query_pos[:, None] - key_pos[None, :] + length - 1]
    onehot = (bucket_ids[:, :, None] == jnp.arange(table_low.shape[0], dtype=jnp.int32)).astype(
        jnp.bfloat16
    )
    score_bias = jnp.einsum("qkn,nh->hqk", onehot, table_low, preferred_element_type=jnp.float32)
    return (onehot, score_bias)


def split_heads(values, head_count):
    return values.reshape(
        values.shape[0], values.shape[1], head_count, values.shape[2] // head_count
    )


def masked_scores(queries, keys_all, score_bias, seg_query, seg_key, score_scale):
    raw = (
        jnp.einsum("bqhd,bkhd->bhqk", queries, keys_all, preferred_element_type=jnp.float32)
        * score_scale
        + score_bias[None]
    )
    same = seg_query[:, None, :, None] == seg_key[:, None, None, :]
    return jnp.where(same, raw, masked_score)


def on_device(
    tokens,
    attn_qkv,
    attn_out,
    norm_gains,
    router,
    rel_table,
    w_in,
    w_out,
    cotangent,
    segments,
    buckets,
    expert_ids,
    slots,
):
    ctx_count = lax.axis_size("ctx")
    ctx_index = lax.axis_index("ctx")
    block_len = tokens.shape[1]
    model_width = tokens.shape[2]
    length = ctx_count * block_len
    head_count = H
    score_scale = DH ** (-0.5)
    local_experts = w_in.shape[0]
    experts = local_experts * ctx_count
    group_rows = SEQ_MB * block_len
    capacity = group_rows * 4 // (3 * experts)
    slot_total = experts * capacity
    query_start = ctx_index * block_len
    expert_range = jnp.arange(experts, dtype=jnp.int32)
    acc_qkv = jnp.zeros((3, model_width, model_width), jnp.float32)
    acc_out = jnp.zeros((model_width, model_width), jnp.float32)
    acc_gains = jnp.zeros((2, model_width), jnp.float32)
    acc_router = jnp.zeros((model_width, experts), jnp.float32)
    acc_table = jnp.zeros((NB, head_count), jnp.float32)
    acc_win = jnp.zeros((local_experts, model_width, FF), jnp.float32)
    acc_wout = jnp.zeros((local_experts, FF, model_width), jnp.float32)
    outputs = []
    input_grads = []
    for micro_step in range(MICRO):
        seq_start = micro_step * SEQ_MB
        qkv_full, out_full, gains_full, router_full, table_flat = gather_layer(
            attn_qkv, attn_out, norm_gains, router, rel_table
        )
        win_full, wout_full = gather_experts(w_in, w_out)
        table_low = table_flat.reshape(NB, head_count)
        batch_x = tokens[seq_start : seq_start + SEQ_MB]
        batch_cot = cotangent[seq_start : seq_start + SEQ_MB]
        batch_seg = segments[seq_start : seq_start + SEQ_MB]
        batch_ids = expert_ids[seq_start : seq_start + SEQ_MB]
        batch_slots = slots[seq_start : seq_start + SEQ_MB]
        batch_live = batch_seg >= 0
        x_float = batch_x.astype(jnp.float32)
        gain_first = gains_full[0].astype(jnp.float32)
        gain_second = gains_full[1].astype(jnp.float32)
        normed = rms_scale(x_float, gain_first).astype(jnp.bfloat16)
        projected = jnp.einsum(
            "bsd,pde->pbse", normed, qkv_full, preferred_element_type=jnp.float32
        ).astype(jnp.bfloat16)
        keys_all, values_all, seg_all = (
            lax.all_gather(projected[1], "ctx", axis=1, tiled=True),
            lax.all_gather(projected[2], "ctx", axis=1, tiled=True),
            lax.all_gather(batch_seg, "ctx", axis=1, tiled=True),
        )
        onehot, score_bias = bias_block(buckets, table_low, query_start, block_len, length, length)
        queries4 = split_heads(projected[0], head_count)
        keys4 = split_heads(keys_all, head_count)
        values4 = split_heads(values_all, head_count)
        scores = masked_scores(queries4, keys4, score_bias, batch_seg, seg_all, score_scale)
        row_peak = jnp.max(scores, axis=-1, keepdims=True)
        shifted = jnp.exp(scores - row_peak)
        row_total = jnp.sum(shifted, axis=-1, keepdims=True)
        prob_low = (shifted / row_total).astype(jnp.bfloat16)
        log_total = row_peak + jnp.log(row_total)
        mixed_low = (
            jnp.einsum("bhqk,bkhd->bqhd", prob_low, values4, preferred_element_type=jnp.float32)
            .reshape(SEQ_MB, block_len, model_width)
            .astype(jnp.bfloat16)
        )
        branch = jnp.einsum("bsd,de->bse", mixed_low, out_full, preferred_element_type=jnp.float32)
        hidden = x_float + branch
        normed2 = rms_scale(hidden, gain_second).astype(jnp.bfloat16)
        logits = jnp.einsum("bsd,de->bse", normed2, router_full, preferred_element_type=jnp.float32)
        gate_probs = jax.nn.softmax(logits, axis=-1)
        pick_mask = (batch_ids[..., None] == expert_range).astype(jnp.float32)
        chosen = jnp.sum(gate_probs * pick_mask, axis=-1)
        kept_rows = ((batch_slots < capacity) & batch_live).reshape(group_rows)
        slot_codes = (batch_ids * capacity + batch_slots).reshape(group_rows)
        target = jnp.where(kept_rows, slot_codes, slot_total)
        safe_codes = jnp.minimum(target, slot_total - 1)
        send_rows = (
            jnp.zeros((slot_total, model_width), jnp.bfloat16)
            .at[target]
            .set(normed2.reshape(group_rows, model_width), mode="drop")
        )
        arrived = lax.all_to_all(
            send_rows.reshape(experts, capacity, model_width),
            "ctx",
            split_axis=0,
            concat_axis=1,
            tiled=True,
        )
        expert_pre = jnp.einsum(
            "erd,edf->erf", arrived, win_full, preferred_element_type=jnp.float32
        )
        expert_act = gelu_tanh(expert_pre).astype(jnp.bfloat16)
        produced = jnp.einsum(
            "erf,efd->erd", expert_act, wout_full, preferred_element_type=jnp.float32
        ).astype(jnp.bfloat16)
        returned = lax.all_to_all(produced, "ctx", split_axis=1, concat_axis=0, tiled=True)
        picked_low = returned.reshape(slot_total, model_width)[safe_codes]
        picked = (
            jnp.where(kept_rows[:, None], picked_low, jnp.zeros_like(picked_low))
            .astype(jnp.float32)
            .reshape(SEQ_MB, block_len, model_width)
        )
        result = hidden + chosen[..., None] * picked
        outputs.append(result.astype(jnp.bfloat16))
        qkv_full, out_full, gains_full, router_full, table_flat = gather_layer(
            attn_qkv, attn_out, norm_gains, router, rel_table
        )
        win_full, wout_full = gather_experts(w_in, w_out)
        table_low = table_flat.reshape(NB, head_count)
        grad_out = batch_cot.astype(jnp.float32) * batch_live[..., None].astype(jnp.float32)
        grad_picked = (
            (chosen[..., None] * grad_out).astype(jnp.bfloat16).reshape(group_rows, model_width)
        )
        grad_chosen = jnp.sum(grad_out * picked, axis=-1)
        grad_logits = gate_probs * (
            grad_chosen[..., None] * pick_mask - (grad_chosen * chosen)[..., None]
        )
        acc_router = acc_router + jnp.einsum(
            "bsd,bse->de", normed2.astype(jnp.float32), grad_logits, precision=precise
        )
        grad_normed2 = jnp.einsum(
            "bse,de->bsd", grad_logits, router_full.astype(jnp.float32), precision=precise
        )
        send_grad = (
            jnp.zeros((slot_total, model_width), jnp.bfloat16)
            .at[target]
            .set(grad_picked, mode="drop")
        )
        grad_arrived = lax.all_to_all(
            send_grad.reshape(experts, capacity, model_width),
            "ctx",
            split_axis=0,
            concat_axis=1,
            tiled=True,
        )
        acc_wout = acc_wout + jnp.einsum(
            "erf,erd->efd", expert_act, grad_arrived, preferred_element_type=jnp.float32
        )
        grad_act = jnp.einsum(
            "erd,efd->erf", grad_arrived, wout_full, preferred_element_type=jnp.float32
        )
        gelu_pull = jax.vjp(gelu_tanh, expert_pre)[1]
        grad_pre = gelu_pull(grad_act)[0].astype(jnp.bfloat16)
        acc_win = acc_win + jnp.einsum(
            "erd,erf->edf", arrived, grad_pre, preferred_element_type=jnp.float32
        )
        grad_sent = jnp.einsum(
            "erf,edf->erd", grad_pre, win_full, preferred_element_type=jnp.float32
        ).astype(jnp.bfloat16)
        grad_home = lax.all_to_all(grad_sent, "ctx", split_axis=1, concat_axis=0, tiled=True)
        home_rows = grad_home.reshape(slot_total, model_width)[safe_codes]
        grad_expert_in = jnp.where(kept_rows[:, None], home_rows, jnp.zeros_like(home_rows)).astype(
            jnp.float32
        )
        grad_normed2 = grad_normed2 + grad_expert_in.reshape(SEQ_MB, block_len, model_width)
        second_pull = jax.vjp(rms_scale, hidden, gain_second)[1]
        grad_hidden_norm, grad_gain_second = second_pull(grad_normed2)
        grad_hidden = grad_out + grad_hidden_norm
        grad_branch = grad_hidden.astype(jnp.bfloat16)
        acc_out = acc_out + jnp.einsum(
            "bsd,bse->de", mixed_low, grad_branch, preferred_element_type=jnp.float32
        )
        grad_mixed = jnp.einsum(
            "bse,de->bsd", grad_branch, out_full, preferred_element_type=jnp.float32
        ).astype(jnp.bfloat16)
        grad_mixed4 = split_heads(grad_mixed, head_count)
        onehot, score_bias = bias_block(buckets, table_low, query_start, block_len, length, length)
        scores = masked_scores(queries4, keys4, score_bias, batch_seg, seg_all, score_scale)
        prob_rows = jnp.exp(scores - log_total)
        grad_probs = jnp.einsum(
            "bqhd,bkhd->bhqk", grad_mixed4, values4, preferred_element_type=jnp.float32
        )
        row_delta = jnp.sum(prob_rows * grad_probs, axis=-1, keepdims=True)
        grad_scores = (prob_rows * (grad_probs - row_delta)).astype(jnp.bfloat16)
        grad_queries = (
            (
                jnp.einsum(
                    "bhqk,bkhd->bqhd", grad_scores, keys4, preferred_element_type=jnp.float32
                )
                * score_scale
            )
            .reshape(SEQ_MB, block_len, model_width)
            .astype(jnp.bfloat16)
        )
        acc_table = acc_table + jnp.einsum(
            "qkn,bhqk->nh", onehot, grad_scores, preferred_element_type=jnp.float32
        )
        key_part = (
            jnp.einsum("bhqk,bqhd->bkhd", grad_scores, queries4, preferred_element_type=jnp.float32)
            * score_scale
        )
        value_part = jnp.einsum(
            "bhqk,bqhd->bkhd",
            prob_rows.astype(jnp.bfloat16),
            grad_mixed4,
            preferred_element_type=jnp.float32,
        )
        key_sum, value_sum = (
            lax.psum_scatter(
                key_part.reshape(SEQ_MB, length, model_width),
                "ctx",
                scatter_dimension=1,
                tiled=True,
            ),
            lax.psum_scatter(
                value_part.reshape(SEQ_MB, length, model_width),
                "ctx",
                scatter_dimension=1,
                tiled=True,
            ),
        )
        grad_keys = key_sum.astype(jnp.bfloat16)
        grad_values = value_sum.astype(jnp.bfloat16)
        grad_stack = jnp.stack([grad_queries, grad_keys, grad_values])
        acc_qkv = acc_qkv + jnp.einsum(
            "bsd,pbse->pde", normed, grad_stack, preferred_element_type=jnp.float32
        )
        grad_normed = jnp.einsum(
            "pbse,pde->bsd", grad_stack, qkv_full, preferred_element_type=jnp.float32
        )
        first_pull = jax.vjp(rms_scale, x_float, gain_first)[1]
        grad_x_norm, grad_gain_first = first_pull(grad_normed)
        input_grads.append(grad_hidden + grad_x_norm)
        acc_gains = acc_gains + jnp.stack([grad_gain_first, grad_gain_second])
    layer_sums = (
        lax.psum_scatter(acc_qkv, ("dp", "ctx"), scatter_dimension=1, tiled=True),
        lax.psum_scatter(acc_out, ("dp", "ctx"), scatter_dimension=0, tiled=True),
        lax.psum_scatter(acc_gains, ("dp", "ctx"), scatter_dimension=1, tiled=True),
        lax.psum_scatter(acc_router, ("dp", "ctx"), scatter_dimension=0, tiled=True),
        lax.psum_scatter(
            acc_table.reshape(NB * head_count), ("dp", "ctx"), scatter_dimension=0, tiled=True
        ),
    )
    expert_sums = (
        lax.psum_scatter(
            acc_win.astype(jnp.bfloat16), "dp", scatter_dimension=1, tiled=True
        ).astype(jnp.float32),
        lax.psum_scatter(
            acc_wout.astype(jnp.bfloat16), "dp", scatter_dimension=1, tiled=True
        ).astype(jnp.float32),
    )
    return (
        jnp.concatenate(outputs, axis=0),
        jnp.concatenate(input_grads, axis=0),
        layer_sums[0],
        layer_sums[1],
        layer_sums[2],
        layer_sums[3],
        layer_sums[4],
        expert_sums[0],
        expert_sums[1],
    )


def solution(mesh):
    in_specs = (
        P("dp", "ctx", None),
        P(None, ("dp", "ctx"), None),
        P(("dp", "ctx"), None),
        P(None, ("dp", "ctx")),
        P(("dp", "ctx"), None),
        P(("dp", "ctx")),
        P("ctx", "dp", None),
        P("ctx", "dp", None),
        P("dp", "ctx", None),
        P("dp", "ctx"),
        P(),
        P("dp", "ctx"),
        P("dp", "ctx"),
    )
    out_specs = (
        P("dp", "ctx", None),
        P("dp", "ctx", None),
        P(None, ("dp", "ctx"), None),
        P(("dp", "ctx"), None),
        P(None, ("dp", "ctx")),
        P(("dp", "ctx"), None),
        P(("dp", "ctx")),
        P("ctx", "dp", None),
        P("ctx", "dp", None),
    )
    return jax.shard_map(
        on_device, mesh=mesh, in_specs=in_specs, out_specs=out_specs, check_vma=False
    )
```

profile of v0, /device:TPU:0, one launch (start us, length us, event | category | flops | bytes accessed | tf_op | source)
XLA Modules:
  0.0 1830.0 jit_solution(2247360829778107737)
XLA Ops:
  8.0 43.3 %all-gather.4 = bf16[32,24,2]{1,2,0:T(2,128)(2,1)S(1)} all-gather(bf16[1,24,2]{1,2,0:T(2,128)(2,1)} %bitcast.418), channel_id=1, replica_groups=mesh['dp'=4,'ctx'=8] {'dp','ctx'}, dimensions={0}, use_global_device_ids=true | all-gather | bytes 3168 | tf_op jit(solution)/shard_map/all_gather | solution.py:33
  54.3 19.5 %all-gather.15.cloned.1.call-done = bf16[3,768,768]{2,1,0:T(8,128)(2,1)} async-done(((bf16[3,24,768]{2,1,0:T(8,128)(2,1)}), bf16[3,768,768]{2,1,0:T(8,128)(2,1)}) %all-gather.15.cloned.1.call-update) | async-done | bytes 3538960 | tf_op jit(solution)/shard_map/all_gather | solution.py:31
  87.0 9.4 all_gather.74
  96.4 9.1 all_gather.65
  105.8 724.9 %gather_fusion = s32[131072]{0:T(1024)S(1)} fusion(s32[2047]{0:T(1024)S(1)} %copy-done, s32[131072]{0:T(1024)S(1)} %broadcast_clamp_fusion), kind=kCustom, calls=%fused_computation | custom fusion | bytes 1572864 | tf_op jit(solution)/shard_map/gather | solution.py:49
  837.3 38.7 %all-reduce = bf16[384]{0:T(512)(128)(2,1)S(1)} all-reduce(bf16[384]{0:T(512)(128)(2,1)S(1)} %dynamic-update-slice), channel_id=1, replica_groups=mesh['dp'=4,'ctx'=8] {'dp','ctx'}, use_global_device_ids=true, to_apply=%add | all-reduce | flops 384 | bytes 1536
  876.1 40.9 %all-gather.5 = bf16[32,24,8]{1,2,0:T(8,128)(2,1)S(1)} all-gather(bf16[1,24,8]{1,2,0:T(8,128)(2,1)S(1)} %bitcast.417), channel_id=1, replica_groups=mesh['dp'=4,'ctx'=8] {'dp','ctx'}, dimensions={0}, use_global_device_ids=true | all-gather | bytes 12672 | tf_op jit(solution)/shard_map/all_gather | solution.py:34
  917.8 23.4 %copy.117 = pred[128,1024,32]{1,2,0:T(32,128)(4,1)S(1)} copy(pred[128,1024,32]{0,2,1:T(32,128)(4,1)} %iota_compare_fusion) | data formatting | bytes 8388608 | tf_op jit(solution)/shard_map/eq | solution.py:50
  941.7 4.5 fusion.152
  956.7 8.2 fusion.205
  972.2 8.2 fusion.204
  994.1 4.8 all-to-all-done
  1009.6 15.4 all-to-all-start.2
  1054.9 4.7 fusion.40
  1063.4 6.3 fusion.47
  1092.0 4.7 all-to-all-start.7
  1126.6 5.8 fusion.28
  1159.4 5.2 multiply_reduce_fusion
  1185.8 44.4 %reduce-scatter.16.cloned.1.call-done = f32[1,128,768]{2,1,0:T(8,128)} async-done(((f32[1,1024,768]{2,1,0:T(8,128)}), f32[1,128,768]{2,1,0:T(8,128)}) %reduce-scatter.16.cloned.1.call-update) | async-done | bytes 393232 | tf_op jit(solution)/shard_map/reduce_scatter | solution.py:290
  1231.9 48.0 %reduce-scatter.10.cloned.1.call-done = f32[1,128,768]{2,1,0:T(8,128)} async-done(((f32[1,1024,768]{2,1,0:T(8,128)}), f32[1,128,768]{2,1,0:T(8,128)}) %reduce-scatter.10.cloned.1.call-update) | async-done | bytes 393232 | tf_op jit(solution)/shard_map/reduce_scatter | solution.py:284
  1281.6 5.1 fusion.115
  1286.7 43.1 %reduce-scatter.14.cloned.1.call-done = f32[1,128,768]{2,1,0:T(8,128)} async-done(((f32[1,1024,768]{2,1,0:T(8,128)}), f32[1,128,768]{2,1,0:T(8,128)}) %reduce-scatter.14.cloned.1.call-update) | async-done | bytes 393232 | tf_op jit(solution)/shard_map/reduce_scatter | solution.py:284
  1331.5 7.3 add_bitcast_fusion
  1338.8 11.0 copy.138
  1365.4 6.9 copy.140
  1372.3 7.7 copy.139
  1385.5 4.9 fusion.84
  1407.5 40.7 %all-reduce.5 = (f32[2,768]{1,0:T(2,128)S(1)}, f32[768,8]{0,1:T(8,128)S(1)}, f32[384]{0:T(512)S(1)}) all-reduce(f32[2,768]{1,0:T(2,128)S(1)} %maximum_add_fusion, f32[768,8]{0,1:T(8,128)} %convolution_add_fusion.3, f32[384]{0:T(512)S(1)} %copy-done.101), channel_id=12, replica_groups=mesh['dp'=4,'ctx'=8] {'dp','ctx'}, use_global_device_ids=true, to_apply=%region_36.37.clone | all-reduce | flops 8064 | bytes 64512
  1453.6 87.9 %all-reduce.8.cloned.1.call-done = f32[3,768,768]{2,0,1:T(4,128)} async-done(((f32[3,768,768]{2,0,1:T(4,128)}), f32[3,768,768]{2,0,1:T(4,128)}) %all-reduce.8.cloned.1.call-update) | async-done | bytes 7077904
  1543.2 85.9 %reduce-scatter.22.cloned.1.call-done = bf16[1,768,768]{2,1,0:T(8,128)(2,1)} async-done(((bf16[1,3072,768]{2,1,0:T(8,128)(2,1)}), bf16[1,768,768]{2,1,0:T(8,128)(2,1)}) %reduce-scatter.22.cloned.1.call-update) | async-done | bytes 1179664 | tf_op jit(solution)/shard_map/reduce_scatter | solution.py:323
  1632.0 85.2 %reduce-scatter.20.cloned.1.call-done = bf16[1,192,3072]{2,1,0:T(8,128)(2,1)} async-done(((bf16[1,768,3072]{2,1,0:T(8,128)(2,1)}), bf16[1,192,3072]{2,1,0:T(8,128)(2,1)}) %reduce-scatter.20.cloned.1.call-update) | async-done | bytes 1179664 | tf_op jit(solution)/shard_map/reduce_scatter | solution.py:320
  1720.1 103.2 %reduce-scatter.18.cloned.1.call-done = f32[24,768]{1,0:T(8,128)} async-done(((f32[768,768]{1,0:T(8,128)}), f32[24,768]{1,0:T(8,128)}) %reduce-scatter.18.cloned.1.call-update) | async-done | bytes 73744 | tf_op jit(solution)/shard_map/reduce_scatter | solution.py:312
  (487 shorter events, 255.9 us)
Async XLA Ops:
  7.2 66.6 %all-gather.15.cloned.1.call-start = ((), (), s32[]{:S(2)}) async-start(), calls=%async_computation.15 | async-start | bytes 3649536 | tf_op jit(solution)/shard_map/all_gather | solution.py:31
  7.9 938.7 %all-gather.29.cloned.1.call-start = ((), (), s32[]{:S(2)}) async-start(), calls=%async_computation.29 | async-start | bytes 1769472 | tf_op jit(solution)/shard_map/all_gather | solution.py:132
  77.6 870.8 %all-gather.27.cloned.1.call-start = ((), (), s32[]{:S(2)}) async-start(), calls=%async_computation.28 | async-start | bytes 1769472 | tf_op jit(solution)/shard_map/all_gather | solution.py:133
  78.3 873.3 %all-gather.25.cloned.1.call-start = ((), (), s32[]{:S(2)}) async-start(), calls=%async_computation.27 | async-start | bytes 1769472 | tf_op jit(solution)/shard_map/all_gather | solution.py:132
  81.5 871.9 %all-gather.23.cloned.1.call-start = ((), (), s32[]{:S(2)}) async-start(), calls=%async_computation.26 | async-start | bytes 1769472 | tf_op jit(solution)/shard_map/all_gather | solution.py:133
  82.1 887.7 %all-gather.17.cloned.1.call-start = ((), (), s32[]{:S(2)}) async-start(), calls=%async_computation.16 | async-start | bytes 1216512 | tf_op jit(solution)/shard_map/all_gather | solution.py:32
  82.7 942.4 %all-gather.19.cloned.1.call-start = ((), (), s32[]{:S(2)}) async-start(), calls=%async_computation.17 | async-start | bytes 5898240 | tf_op jit(solution)/shard_map/all_gather | solution.py:41
  83.4 952.7 %all-gather.21.cloned.1.call-start = ((), (), s32[]{:S(2)}) async-start(), calls=%async_computation.18 | async-start | bytes 5898240 | tf_op jit(solution)/shard_map/all_gather | solution.py:42
  831.1 110.1 %copy-start.34 = (s32[128,1024]{0,1:T(8,128)}, s32[128,1024]{0,1:T(8,128)S(1)}, u32[]{:S(2)}) copy-start(s32[128,1024]{0,1:T(8,128)S(1)} %copy.115) | copy-start | bytes 1572868
  837.0 155.0 %copy-start.135 = (s32[128]{0:T(128)}, s32[128]{0:T(128)S(1)}, u32[]{:S(2)}) copy-start(s32[128]{0:T(128)S(1)} %fusion.181) | copy-start | bytes 1540
  988.3 10.6 all-to-all-start
  991.9 128.7 %copy-start.65 = (f32[128,8]{0,1:T(8,128)}, f32[128,8]{0,1:T(8,128)S(1)}, u32[]{:S(2)}) copy-start(f32[128,8]{0,1:T(8,128)S(1)} %get-tuple-element.107) | copy-start | bytes 12292
  998.9 10.6 all-to-all-start.6
  1002.5 118.5 %copy-start.67 = (f32[128,8]{0,1:T(8,128)}, f32[128,8]{0,1:T(8,128)S(1)}, u32[]{:S(2)}) copy-start(f32[128,8]{0,1:T(8,128)S(1)} %get-tuple-element.105) | copy-start | bytes 12292
  1009.6 22.4 %all-to-all-start.2 = ((bf16[8,21,768]{2,1,0:T(8,128)(2,1)}), bf16[8,21,768]{2,1,0:T(8,128)(2,1)}, u32[]{:S(2)}, u32[]{:S(2)}) async-start(bf16[8,21,768]{2,1,0:T(8,128)(2,1)} %reshape.1202), calls=%async_computation.2 | async-start | bytes 589824 | tf_op jit(solution)/shard_map/all_to_all | solution.py:167
  1032.0 17.0 all-to-all-start.4
  1049.1 27.5 %all-to-all-start.1 = ((bf16[8,2,8064]{2,1,0:T(2,128)(2,1)}), bf16[8,2,8064]{2,1,0:T(2,128)(2,1)}, u32[]{:S(2)}, u32[]{:S(2)}) async-start(bf16[8,2,8064]{2,1,0:T(2,128)(2,1)} %reshape.1338), calls=%async_computation.1 | async-start | bytes 516096 | tf_op jit(solution)/shard_map/all_to_all | solution.py:181
  1076.6 15.4 all-to-all-start.5
  1092.0 11.9 all-to-all-start.7
  1103.9 11.2 all-to-all-start.3
  1108.1 76.1 %reduce-scatter.12.cloned.1.call-start = ((), (), s32[]{:S(2)}) async-start(), calls=%async_computation.20 | async-start | bytes 3538944 | tf_op jit(solution)/shard_map/reduce_scatter | solution.py:290
  1136.0 94.3 %reduce-scatter.16.cloned.1.call-start = ((), (), s32[]{:S(2)}) async-start(), calls=%async_computation.22 | async-start | bytes 3538944 | tf_op jit(solution)/shard_map/reduce_scatter | solution.py:290
  1144.2 135.7 %reduce-scatter.10.cloned.1.call-start = ((), (), s32[]{:S(2)}) async-start(), calls=%async_computation.19 | async-start | bytes 3538944 | tf_op jit(solution)/shard_map/reduce_scatter | solution.py:284
  1159.3 170.5 %reduce-scatter.14.cloned.1.call-start = ((), (), s32[]{:S(2)}) async-start(), calls=%async_computation.21 | async-start | bytes 3538944 | tf_op jit(solution)/shard_map/reduce_scatter | solution.py:284
  1174.6 366.9 %all-reduce.8.cloned.1.call-start = ((), (), s32[]{:S(2)}) async-start(), calls=%async_computation.30 | async-start | bytes 18874368
  1179.0 102.6 %copy-start.12 = (bf16[2,128,768]{2,1,0:T(8,128)(2,1)S(1)}, bf16[2,128,768]{2,1,0:T(8,128)(2,1)}, u32[]{:S(2)}) copy-start(bf16[2,128,768]{2,1,0:T(8,128)(2,1)} %param.13) | copy-start | bytes 1179652
  1179.0 102.6 %copy-start.64 = (f32[768]{0:T(1024)S(1)}, f32[768]{0:T(1024)}, u32[]{:S(2)}) copy-start(f32[768]{0:T(1024)} %copy-done.63) | copy-start | bytes 9220
  1179.0 102.6 %copy-start.118 = (f32[128]{0:T(128)S(1)}, f32[128]{0:T(128)}, u32[]{:S(2)}) copy-start(f32[128]{0:T(128)} %copy-done.117) | copy-start | bytes 1540
  1349.9 279.3 %reduce-scatter.22.cloned.1.call-start = ((), (), s32[]{:S(2)}) async-start(), calls=%async_computation.25 | async-start | bytes 5898240 | tf_op jit(solution)/shard_map/reduce_scatter | solution.py:323
  1357.8 359.3 %reduce-scatter.20.cloned.1.call-start = ((), (), s32[]{:S(2)}) async-start(), calls=%async_computation.24 | async-start | bytes 5898240 | tf_op jit(solution)/shard_map/reduce_scatter | solution.py:320
  1365.2 458.1 %reduce-scatter.18.cloned.1.call-start = ((), (), s32[]{:S(2)}) async-start(), calls=%async_computation.23 | async-start | bytes 2433024 | tf_op jit(solution)/shard_map/reduce_scatter | solution.py:312
  1542.5 280.8 %copy-start.1 = (s32[2047]{0:T(1024)S(1)}, s32[2047]{0:T(1024)}, u32[]{:S(2)}) copy-start(s32[2047]{0:T(1024)} %param.23) | copy-start | bytes 24568
  (130 other events, 1222.9 us)
Sparse Core Ops, SparseCore 0:
  11.0 62.7 all-gather.14
  77.7 24.4 all-gather.28
  104.1 25.6 all-gather.26
  132.2 25.6 all-gather.24
  160.2 25.6 all-gather.22
  188.7 54.0 all-gather.16
  244.4 88.3 all-gather.18
  334.3 87.8 all-gather.20
  1136.1 44.2 reduce-scatter.11
  1184.0 46.2 reduce-scatter.15
  1233.6 46.2 reduce-scatter.9
  1283.5 46.2 reduce-scatter.13
  1350.0 191.4 all-reduce.7
  1543.8 85.3 reduce-scatter.21
  1631.4 85.7 reduce-scatter.19
  1723.7 99.4 reduce-scatter.17
where the time goes:
time: 1840 us; the launch traced here: 1830 us
  local copies, waits for them, and re-layouts  850 us (46%)
  waiting for transfers between devices  532 us (29%)
  blocking collectives  182 us (10%)
  matrix products  146 us (8%)
  other arithmetic  58.5 us (3%)
  starting transfers between devices  44.3 us (2%)
    gather x3, local copies, waits for them, and re-layouts, bias_block(): bucket_ids = buckets[query_pos[:, None] - key_pos[None, :] + length - 1]  725 us
    reduce_scatter x1, waiting for transfers between devices, on_device(): lax.psum_scatter(acc_out, ('dp', 'ctx'), scatter_dimension=0, tiled=True)  103 us
    unnamed x17, waiting for transfers between devices  91.9 us
    reduce_scatter x2, waiting for transfers between devices, on_device(): lax.psum_scatter(key_part.reshape(SEQ_MB, length, model_width), 'ctx', sc...  91.1 us
    reduce_scatter x1, waiting for transfers between devices, on_device(): lax.psum_scatter(acc_wout.astype(jnp.bfloat16), 'dp', scatter_dimension=1...  85.9 us
    reduce_scatter x1, waiting for transfers between devices, on_device(): lax.psum_scatter(acc_win.astype(jnp.bfloat16), 'dp', scatter_dimension=1,...  85.2 us
    unnamed x2, blocking collectives  79.4 us
    reduce_scatter x2, waiting for transfers between devices, on_device(): lax.psum_scatter(value_part.reshape(SEQ_MB, length, model_width), 'ctx',...  44.4 us
  transfers between devices with their start and end apart: 24, of which 12 were waited for; matrix products, arithmetic and copies ran while one was open for 55% of the time, Pallas kernels for 0%

commit v1 on v0

v1 whole, which is shorter than its diff:
```python
import jax
import jax.numpy as jnp
from jax import lax
from jax.experimental import pallas as pl
from jax.experimental.pallas import tpu as pltpu
from jax.sharding import PartitionSpec as P

H = 12
DH = 64
FF = 3072
NB = 32

epsilon = 1e-06
precise = lax.Precision.HIGHEST
masked_score = -1000000000.0
bf16 = jnp.bfloat16
f32 = jnp.float32
VMEM_LIMIT = 50 * 1024 * 1024


def rms_scale(values, gain_row):
    return (
        values * lax.rsqrt(jnp.mean(values * values, axis=-1, keepdims=True) + epsilon) * gain_row
    )


def gelu_tanh(values):
    return jax.nn.gelu(values, approximate=True)


def dot(a, b, ca, cb):
    return lax.dot_general(a, b, (((ca,), (cb,)), ((), ())), preferred_element_type=f32)


def attend_kernel(qkv_ref, base_ref, segq_ref, segk_ref, p_ref, mixed_ref, bias_ref):
    length = qkv_ref.shape[3]
    block = bias_ref.shape[0]
    bias_ref[0:8, :] = base_ref[0]
    rows = 8
    while rows < block:
        bias_ref[rows : 2 * rows, :] = pltpu.roll(bias_ref[0:rows, :], rows, 1)
        rows *= 2
    keys = qkv_ref[1, 0]
    vals = qkv_ref[2, 0]
    seg_keys = segk_ref[...]

    def step(b, carry):
        at = pl.ds(pl.multiple_of(b * block, block), block)
        shift = pl.ds(pl.multiple_of(length - block - b * block, block), length)
        scores = dot(qkv_ref[0, 0, :, at], keys, 0, 0) + bias_ref[:, shift]
        scores = jnp.where(segq_ref[at, :] == seg_keys, scores, masked_score)
        peak = jnp.max(scores, axis=-1, keepdims=True)
        shifted = jnp.exp(scores - peak)
        total = jnp.sum(shifted, axis=-1, keepdims=True)
        probs = (shifted * (1.0 / total)).astype(bf16)
        p_ref[0, at, :] = probs
        mixed_ref[b, 0] = dot(vals, probs, 1, 1).astype(bf16)
        return carry

    lax.fori_loop(0, length // block, step, 0)


def attend(qkv, base, seg, block):
    heads, length = qkv.shape[1], qkv.shape[3]
    count = length // block
    return pl.pallas_call(
        attend_kernel,
        grid=(heads,),
        in_specs=[
            pl.BlockSpec((3, 1, DH, length), lambda h: (0, h, 0, 0)),
            pl.BlockSpec((1, 8, 2 * length), lambda h: (h, 0, 0)),
            pl.BlockSpec((length, 1), lambda h: (0, 0)),
            pl.BlockSpec((1, length), lambda h: (0, 0)),
        ],
        out_specs=[
            pl.BlockSpec((1, length, length), lambda h: (h, 0, 0)),
            pl.BlockSpec((count, 1, DH, block), lambda h: (0, h, 0, 0)),
        ],
        out_shape=[
            jax.ShapeDtypeStruct((heads, length, length), bf16),
            jax.ShapeDtypeStruct((count, heads, DH, block), bf16),
        ],
        scratch_shapes=[pltpu.VMEM((block, 2 * length), f32)],
        compiler_params=pltpu.CompilerParams(vmem_limit_bytes=VMEM_LIMIT),
        cost_estimate=pl.CostEstimate(
            flops=4 * heads * length * length * DH,
            bytes_accessed=2 * heads * length * length,
            transcendentals=heads * length * length,
        ),
    )(qkv, base, seg[:, None], seg[None, :])


def attend_back_kernel(qkv_ref, p_ref, gm_ref, g_ref, diag_ref, acc_ref, gk_ref, gv_ref):
    length = qkv_ref.shape[3]
    block = acc_ref.shape[0]
    acc_ref[...] = jnp.zeros_like(acc_ref)
    gk_ref[...] = jnp.zeros_like(gk_ref)
    gv_ref[...] = jnp.zeros_like(gv_ref)
    keys = qkv_ref[1, 0]
    vals = qkv_ref[2, 0]

    def step(b, carry):
        at = pl.ds(pl.multiple_of(b * block, block), block)
        shift = pl.ds(pl.multiple_of(length - block - b * block, block), length)
        gm = gm_ref[b, 0]
        probs_low = p_ref[0, at, :]
        probs = probs_low.astype(f32)
        weighed = probs * dot(gm, vals, 0, 0)
        delta = jnp.sum(weighed, axis=-1, keepdims=True)
        gs = weighed - probs * delta
        gs_low = gs.astype(bf16)
        acc_ref[:, shift] += gs
        g_ref[0, 0, :, at] = (dot(keys, gs_low, 1, 1) * (DH**-0.5)).astype(bf16)
        gk_ref[...] += dot(qkv_ref[0, 0, :, at], gs_low, 1, 0)
        gv_ref[...] += dot(gm, probs_low, 1, 0)
        return carry

    lax.fori_loop(0, length // block, step, 0)
    g_ref[1, 0] = gk_ref[...].astype(bf16)
    g_ref[2, 0] = gv_ref[...].astype(bf16)
    rows = block // 2
    while rows >= 8:
        acc_ref[0:rows, :] += pltpu.roll(acc_ref[rows : 2 * rows, :], 2 * length - rows, 1)
        rows //= 2
    diag_ref[0] = acc_ref[0:8, :]


def attend_back(qkv, probs, gm):
    heads, length = qkv.shape[1], qkv.shape[3]
    count, block = gm.shape[0], gm.shape[3]
    return pl.pallas_call(
        attend_back_kernel,
        grid=(heads,),
        in_specs=[
            pl.BlockSpec((3, 1, DH, length), lambda h: (0, h, 0, 0)),
            pl.BlockSpec((1, length, length), lambda h: (h, 0, 0)),
            pl.BlockSpec((count, 1, DH, block), lambda h: (0, h, 0, 0)),
        ],
        out_specs=[
            pl.BlockSpec((3, 1, DH, length), lambda h: (0, h, 0, 0)),
            pl.BlockSpec((1, 8, 2 * length), lambda h: (h, 0, 0)),
        ],
        out_shape=[
            jax.ShapeDtypeStruct((3, heads, DH, length), bf16),
            jax.ShapeDtypeStruct((heads, 8, 2 * length), f32),
        ],
        scratch_shapes=[
            pltpu.VMEM((block, 2 * length), f32),
            pltpu.VMEM((DH, length), f32),
            pltpu.VMEM((DH, length), f32),
        ],
        compiler_params=pltpu.CompilerParams(vmem_limit_bytes=VMEM_LIMIT),
        cost_estimate=pl.CostEstimate(
            flops=8 * heads * length * length * DH,
            bytes_accessed=2 * heads * length * length,
            transcendentals=0,
        ),
    )(qkv, probs, gm)


def pad_last(values, size):
    widths = [(0, 0)] * (values.ndim - 1) + [(0, size - values.shape[-1])]
    return jnp.pad(values, widths)


def swap(values, axis):
    return lax.all_to_all(values, axis, split_axis=0, concat_axis=0, tiled=True)


def on_device(
    tokens,
    attn_qkv,
    attn_out,
    norm_gains,
    router,
    rel_table,
    w_in,
    w_out,
    cotangent,
    segments,
    buckets,
    expert_ids,
    slots,
):
    ctx_count = lax.axis_size("ctx")
    dp_count = lax.axis_size("dp")
    ctx_index = lax.axis_index("ctx")
    seqs, block, width = tokens.shape
    length = ctx_count * block
    experts = ctx_count * w_in.shape[0]
    own_rows = attn_qkv.shape[1]
    table_rows = rel_table.shape[0]
    groups = ctx_count // seqs
    heads = -(-H // groups)
    cols = heads * DH
    all_cols = groups * cols
    my_seq = ctx_index // groups
    my_group = ctx_index % groups
    capacity = block * 4 // (3 * experts)
    cap_pad = -(-capacity // 8) * 8
    slot_total = experts * cap_pad
    ff_part = FF // dp_count

    qkv_cols = (
        pad_last(attn_qkv, all_cols)
        .reshape(3, own_rows, groups, cols)
        .transpose(2, 1, 0, 3)
        .reshape(groups, own_rows, 3 * cols)
    )
    table_col = jnp.pad(rel_table, (0, own_rows - table_rows))[:, None]
    small = pad_last(jnp.concatenate([norm_gains.T, router, table_col], axis=1), 128)
    packed = jnp.concatenate(
        [qkv_cols, jnp.broadcast_to(small[None], (groups,) + small.shape)], axis=2
    )
    packed = swap(jnp.concatenate([packed] * seqs, axis=0), "ctx")
    layer = lax.all_gather(packed, "dp", axis=0, tiled=False).reshape(width, -1)
    w_heads = layer[:, : 3 * cols]
    rest = layer[:, 3 * cols :]
    gain_first = rest[:, 0].astype(f32)
    gain_second = rest[:, 1].astype(f32)
    router_full = rest[:, 2 : 2 + experts]
    table = rest[:, 2 + experts].reshape(-1, own_rows)[:, :table_rows].reshape(NB, H)

    seg_rows = jnp.pad(
        segments.astype(bf16)[:, None, :], ((0, 0), (0, 15), (0, width - block))
    )
    spread = lax.all_gather(
        jnp.concatenate([tokens, seg_rows], axis=1), "ctx", axis=0, tiled=False
    )
    spread = lax.dynamic_index_in_dim(spread, my_seq, axis=1, keepdims=False)
    x_seq = spread[:, :block].reshape(length, width).astype(f32)
    seg_seq = spread[:, block, :block].reshape(length).astype(jnp.int32)

    out_full = lax.all_gather(attn_out, ("dp", "ctx"), axis=0, tiled=True)
    win_part = swap(
        w_in[0].reshape(-1, dp_count, ff_part).transpose(1, 0, 2), "dp"
    ).reshape(width, ff_part)
    wout_part = w_out[0]

    bucket_line = jnp.pad(jnp.flip(buckets), (0, 1), constant_values=-1)
    onehot_line = (bucket_line[:, None] == jnp.arange(NB, dtype=jnp.int32)).astype(bf16)
    table_part = lax.dynamic_slice_in_dim(
        pad_last(table, groups * heads), my_group * heads, heads, axis=1
    )
    bias_line = jnp.einsum("wn,nh->hw", onehot_line, table_part, preferred_element_type=f32)
    bias_base = jnp.stack(
        [jnp.roll(bias_line, a + 1 - block, axis=1) for a in range(8)], axis=1
    )

    normed_seq = rms_scale(x_seq, gain_first).astype(bf16)
    projected = dot(w_heads, normed_seq, 0, 1).astype(bf16).reshape(3, heads, DH, length)
    scale = jnp.array([DH**-0.5, 1.0, 1.0], bf16)[:, None, None, None]
    projected = projected * scale
    probs, mixed_parts = attend(projected, bias_base, seg_seq, block)
    mixed = swap(mixed_parts.reshape(ctx_count, cols, block), "ctx")
    mixed = mixed.reshape(seqs, all_cols, block)[:, :width]

    live = segments >= 0
    x_float = tokens.astype(f32)
    branch = jnp.einsum("bds,de->bse", mixed, out_full, preferred_element_type=f32)
    hidden = x_float + branch
    normed2 = rms_scale(hidden, gain_second).astype(bf16)
    logits = jnp.einsum("bsd,de->bse", normed2, router_full, preferred_element_type=f32)
    gate_probs = jax.nn.softmax(logits, axis=-1)
    expert_range = jnp.arange(experts, dtype=jnp.int32)
    pick_mask = (expert_ids[..., None] == expert_range).astype(f32)
    chosen = jnp.sum(gate_probs * pick_mask, axis=-1)
    grad_out = cotangent.astype(f32) * live[..., None].astype(f32)
    grad_picked = (chosen[..., None] * grad_out).astype(bf16)
    kept = (slots < capacity) & live
    target = jnp.where(kept, expert_ids * cap_pad + slots, slot_total)
    place = (
        target[:, None, :] == jnp.arange(slot_total, dtype=jnp.int32)[None, :, None]
    ).astype(bf16)

    def to_slots(rows):
        moved = jnp.einsum("bcr,brd->bcd", place, rows, preferred_element_type=f32)
        moved = moved.astype(bf16).reshape(seqs, experts, cap_pad, width)
        return moved.transpose(1, 0, 2, 3).reshape(experts, seqs * cap_pad, width)

    def from_slots(rows):
        rows = rows.reshape(experts, seqs, cap_pad, width).transpose(1, 0, 2, 3)
        rows = rows.reshape(seqs, slot_total, width)
        return jnp.einsum("bcr,bcd->brd", place, rows, preferred_element_type=f32)

    slot_rows = seqs * cap_pad
    arrived = swap(jnp.concatenate([to_slots(normed2), to_slots(grad_picked)], axis=1), "ctx")
    rows_in = lax.all_gather(arrived[:, :slot_rows], "dp", axis=0, tiled=False)
    grads_in = lax.all_gather(arrived[:, slot_rows:], "dp", axis=0, tiled=False)
    rows_in = rows_in.reshape(-1, width)
    grads_in = grads_in.reshape(-1, width)

    expert_pre = dot(rows_in, win_part, 1, 0)
    expert_act = gelu_tanh(expert_pre).astype(bf16)
    produced = lax.psum_scatter(
        dot(expert_act, wout_part, 1, 0).astype(bf16), "dp", scatter_dimension=0, tiled=True
    )
    grad_act = dot(grads_in, wout_part, 1, 1)
    grad_pre = jax.vjp(gelu_tanh, expert_pre)[1](grad_act)[0].astype(bf16)
    grad_sent = lax.psum_scatter(
        dot(grad_pre, win_part, 1, 1).astype(bf16), "dp", scatter_dimension=0, tiled=True
    )
    grad_wout = dot(expert_act, grads_in, 0, 0)
    grad_win = dot(rows_in, grad_pre, 0, 0).astype(bf16)
    grad_win = swap(grad_win.reshape(dp_count, -1, ff_part), "dp").astype(f32)
    grad_win = grad_win.transpose(1, 0, 2).reshape(-1, FF)

    returned = swap(
        jnp.concatenate(
            [
                produced.reshape(ctx_count, slot_rows, width),
                grad_sent.reshape(ctx_count, slot_rows, width),
            ],
            axis=1,
        ),
        "ctx",
    )
    picked = from_slots(returned[:, :slot_rows])
    grad_expert_in = from_slots(returned[:, slot_rows:])
    output = (hidden + chosen[..., None] * picked).astype(bf16)

    grad_chosen = jnp.sum(grad_out * picked, axis=-1)
    grad_logits = gate_probs * (
        grad_chosen[..., None] * pick_mask - (grad_chosen * chosen)[..., None]
    )
    sum_router = jnp.einsum("bsd,bse->de", normed2.astype(f32), grad_logits, precision=precise)
    grad_normed2 = grad_expert_in + jnp.einsum(
        "bse,de->bsd", grad_logits, router_full.astype(f32), precision=precise
    )
    grad_hidden_norm, sum_gain_second = jax.vjp(rms_scale, hidden, gain_second)[1](grad_normed2)
    grad_hidden = grad_out + grad_hidden_norm
    grad_branch = grad_hidden.astype(bf16)
    grad_mixed = jnp.einsum(
        "bse,de->bds", grad_branch, out_full, preferred_element_type=f32
    ).astype(bf16)
    grad_mixed = jnp.pad(grad_mixed, ((0, 0), (0, all_cols - width), (0, 0)))
    grad_mixed = swap(grad_mixed.reshape(ctx_count, cols, block), "ctx")
    sum_out = jnp.einsum("bds,bse->de", mixed, grad_branch, preferred_element_type=f32)
    grad_attn_out = lax.psum_scatter(
        sum_out.astype(bf16), ("dp", "ctx"), scatter_dimension=0, tiled=True
    ).astype(f32)

    grad_parts, diag = attend_back(
        projected, probs, grad_mixed.reshape(ctx_count, heads, DH, block)
    )
    grad_parts = grad_parts.reshape(3 * cols, length)
    normed_part = dot(grad_parts, w_heads, 0, 1).astype(bf16)
    normed_part = swap(normed_part.reshape(ctx_count, block, width), "ctx")
    grad_normed = jnp.sum(
        normed_part.reshape(seqs, groups, block, width).astype(f32), axis=1
    )
    sum_qkv = lax.psum_scatter(
        dot(normed_seq, grad_parts, 0, 1).astype(bf16), "dp", scatter_dimension=0, tiled=True
    )
    sum_qkv = swap(sum_qkv.reshape(ctx_count, own_rows, 3 * cols), "ctx").astype(f32)
    sum_qkv = jnp.sum(sum_qkv.reshape(seqs, groups, own_rows, 3, cols), axis=0)
    grad_attn_qkv = sum_qkv.transpose(2, 1, 0, 3).reshape(3, own_rows, all_cols)[..., :width]

    grad_x_norm, sum_gain_first = jax.vjp(rms_scale, x_float, gain_first)[1](grad_normed)
    grad_tokens = grad_hidden + grad_x_norm

    diag_line = sum(
        jnp.roll(diag[:, a, :], block - 1 - a, axis=1) for a in range(8)
    )
    sum_table = jnp.einsum(
        "wn,hw->nh", onehot_line.astype(f32), diag_line, precision=precise
    )
    sum_table = lax.dynamic_update_slice_in_dim(
        jnp.zeros((NB, groups * heads), f32), sum_table, my_group * heads, axis=1
    )[:, :H]
    table_col = pad_last(sum_table.reshape(-1, table_rows), own_rows).reshape(width, 1)
    sums = lax.psum_scatter(
        jnp.concatenate(
            [sum_gain_first[:, None], sum_gain_second[:, None], sum_router, table_col], axis=1
        ),
        ("dp", "ctx"),
        scatter_dimension=0,
        tiled=True,
    )
    return (
        output,
        grad_tokens,
        grad_attn_qkv,
        grad_attn_out,
        sums[:, :2].T,
        sums[:, 2 : 2 + experts],
        sums[:table_rows, 2 + experts],
        grad_win[None],
        grad_wout[None],
    )


def solution(mesh):
    in_specs = (
        P("dp", "ctx", None),
        P(None, ("dp", "ctx"), None),
        P(("dp", "ctx"), None),
        P(None, ("dp", "ctx")),
        P(("dp", "ctx"), None),
        P(("dp", "ctx")),
        P("ctx", "dp", None),
        P("ctx", "dp", None),
        P("dp", "ctx", None),
        P("dp", "ctx"),
        P(),
        P("dp", "ctx"),
        P("dp", "ctx"),
    )
    out_specs = (
        P("dp", "ctx", None),
        P("dp", "ctx", None),
        P(None, ("dp", "ctx"), None),
        P(("dp", "ctx"), None),
        P(None, ("dp", "ctx")),
        P(("dp", "ctx"), None),
        P(("dp", "ctx")),
        P("ctx", "dp", None),
        P("ctx", "dp", None),
    )
    return jax.shard_map(
        on_device, mesh=mesh, in_specs=in_specs, out_specs=out_specs, check_vma=False
    )
```

time: 1840 us -> 624 us (0.34)
  local copies, waits for them, and re-layouts: 850 us -> 33.3 us
  waiting for transfers between devices: 532 us -> 288 us
  matrix products: 146 us -> 53.5 us
  blocking collectives: 182 us -> 136 us
  Pallas kernels: 0 us -> 39.4 us
  other arithmetic: 58.5 us -> 26.4 us
  starting transfers between devices: 44.3 us -> 23.7 us
    gather x7 -> x0, local copies, waits for them, and re-layouts: 730 us -> none  [the longest x3 725 us: bias_block(): bucket_ids = buckets[query_pos[:, None] - key_pos[None, :] + length - 1]]
    reduce_scatter x7 -> x4, waiting for transfers between devices: 410 us -> 138 us  [the longest x1 50.4 us: on_device(): lax.psum_scatter(dot(grad_pre, win_part, 1, 1).astype(bf16), 'dp', scatte...]
    all_gather x8 -> x5, waiting for transfers between devices: 19.6 us -> 125 us  [the longest x1 39.9 us: on_device(): grads_in = lax.all_gather(arrived[:, slot_rows:], 'dp', axis=0, tiled=False)]
    all_gather x4 -> x0, blocking collectives: 103 us -> none  [the longest x1 43.3 us: gather_layer(): lax.all_gather(norm_gains, ('dp', 'ctx'), axis=1, tiled=True)]
    dot_general x45 -> x20, matrix products: 146 us -> 51.4 us  [the longest x9 39.8 us: dot(): lax.dot_general(a, b, (((ca,), (cb,)), ((), ())), preferred_element_type=...]
    all_to_all x0 -> x3, blocking collectives: none -> 94.5 us  [swap(): return lax.all_to_all(values, axis, split_axis=0, concat_axis=0, tiled=True)]
    unnamed x17 -> x9, waiting for transfers between devices: 91.9 us -> 1.33 us
    pallas_call x0 -> x2, Pallas kernels: none -> 39.4 us  [the longest x1 20.2 us: attend(): pl.pallas_call(attend_kernel, grid=(heads,), in_specs=[pl.BlockSpec((3, 1...]
  transfers between devices with their start and end apart: 24 -> 15, of which waited for: 12 -> 11; matrix products, arithmetic and copies ran while one was open for 55% -> 13% of each run, Pallas kernels for 0% -> 6%
where the time goes in v1:
time: 624 us; the launch traced here: 616 us
  waiting for transfers between devices  288 us (46%)
  blocking collectives  136 us (22%)
  matrix products  53.5 us (9%)
  Pallas kernels  39.4 us (6%)
  local copies, waits for them, and re-layouts  33.3 us (5%)
  other arithmetic  26.4 us (4%)
  starting transfers between devices  23.7 us (4%)
  between operations  15.2 us (2%)
    all_to_all x3, blocking collectives, swap(): return lax.all_to_all(values, axis, split_axis=0, concat_axis=0, tiled=True)  94.5 us
    reduce_scatter x1, waiting for transfers between devices, on_device(): lax.psum_scatter(dot(grad_pre, win_part, 1, 1).astype(bf16), 'dp', scatte...  50.4 us
    reduce_scatter x1, waiting for transfers between devices, on_device(): lax.psum_scatter(sum_out.astype(bf16), ('dp', 'ctx'), scatter_dimension=0...  50.4 us
    unnamed x1, blocking collectives  41.6 us
    all_gather x1, waiting for transfers between devices, on_device(): grads_in = lax.all_gather(arrived[:, slot_rows:], 'dp', axis=0, tiled=False)  39.9 us
    dot_general x9, matrix products, dot(): lax.dot_general(a, b, (((ca,), (cb,)), ((), ())), preferred_element_type=...  39.8 us
    reduce_scatter x1, waiting for transfers between devices, on_device(): lax.psum_scatter(dot(expert_act, wout_part, 1, 0).astype(bf16), 'dp', sca...  37.1 us
    all_gather x1, waiting for transfers between devices, on_device(): lax.all_gather(jnp.concatenate([tokens, seg_rows], axis=1), 'ctx', axis=0...  30.6 us
  transfers between devices with their start and end apart: 15, of which 11 were waited for; matrix products, arithmetic and copies ran while one was open for 13% of the time, Pallas kernels for 6%

profile of v1, /device:TPU:0, one launch (start us, length us, event | category | flops | bytes accessed | tf_op | source)
XLA Modules:
  0.0 615.9 jit_solution(12742183072555298007)
XLA Ops:
  10.3 12.4 %all_to_all.45 = bf16[8,24,704]{2,1,0:T(8,128)(2,1)} all-to-all(bf16[8,24,704]{2,1,0:T(8,128)(2,1)S(1)} %maximum_maximum_fusion), channel_id=1, replica_groups=mesh['dp'=4,'ctx'=8] {'ctx'}, dimensions={0} | all-to-all | bytes 540672 | tf_op jit(solution)/shard_map/all_to_all | solution.py:167
  25.8 26.8 %all-gather.12.cloned.1.call-done = bf16[32,24,704]{2,1,0:T(8,128)(2,1)} async-done(((bf16[8,24,704]{2,1,0:T(8,128)(2,1)}), bf16[32,24,704]{2,1,0:T(8,128)(2,1)}) %all-gather.12.cloned.1.call-update) | async-done | bytes 1081360 | tf_op jit(solution)/shard_map/all_gather | solution.py:216
  57.7 30.6 %all-gather.14.cloned.1.call-done = bf16[16,144,768]{2,1,0:T(8,128)(2,1)} async-done(((bf16[2,144,768]{2,1,0:T(8,128)(2,1)}), bf16[16,144,768]{2,1,0:T(8,128)(2,1)}) %all-gather.14.cloned.1.call-update) | async-done | bytes 3538960 | tf_op jit(solution)/shard_map/all_gather | solution.py:227
  98.2 20.2 %shard_map.205 = (bf16[3,1024,1024]{2,1,0:T(8,128)(2,1)}, bf16[8,3,64,128]{3,2,1,0:T(8,128)(2,1)}) custom-call(bf16[3,3,64,1024]{3,2,1,0:T(8,128)(2,1)S(1)} %broadcast_multiply_fusion.qkv_ref, f32[3,8,2048]{2,1,0:T(8,128)S(1)} %stack.35.base_ref, s32[1024,1]{1,0:T(8,128)S(1)} %copy.106.segq_ref, s32[1,1024]{1,0:T(1,128)S(1)} %get-tuple-element.23.segk_ref), custom_call_target="tpu_custom_call" | custom-call | flops 805306368 | bytes 6291456 | tf_op jit(solution)/shard_map/pallas_call | solution.py:66
  118.4 3.5 all-to-all-start.1
  122.5 22.8 %all-gather.10.cloned.1.call-done = bf16[768,768]{1,0:T(8,128)(2,1)} async-done(((bf16[24,768]{1,0:T(8,128)(2,1)}), bf16[768,768]{1,0:T(8,128)(2,1)}) %all-gather.10.cloned.1.call-update) | async-done | bytes 1179664 | tf_op jit(solution)/shard_map/all_gather | solution.py:234
  155.3 19.3 %all_to_all.46 = bf16[8,96,768]{2,1,0:T(8,128)(2,1)S(1)} all-to-all(bf16[8,96,768]{2,1,0:T(8,128)(2,1)S(1)} %pad_maximum_fusion), channel_id=1, replica_groups=mesh['dp'=4,'ctx'=8] {'ctx'}, dimensions={0} | all-to-all | bytes 2359296 | tf_op jit(solution)/shard_map/all_to_all | solution.py:167
  176.4 3.5 reshape_squeeze.8
  181.3 62.8 %all_to_all.47 = bf16[4,192,768]{2,1,0:T(8,128)(2,1)} all-to-all(bf16[4,192,768]{2,1,0:T(8,128)(2,1)S(1)} %copy.111), channel_id=1, replica_groups=mesh['dp'=4,'ctx'=8] {'dp'}, dimensions={0} | all-to-all | bytes 2359296 | tf_op jit(solution)/shard_map/all_to_all | solution.py:167
  244.2 5.1 all-gather.16.cloned.1.call-done
  249.3 4.0 fusion.76
  255.6 4.4 convolution_convert_fusion.1
  260.0 39.9 %all-gather.18.cloned.1.call-done = bf16[32,48,768]{2,1,0:T(8,128)(2,1)} async-done(((bf16[8,48,768]{2,1,0:T(8,128)(2,1)}), bf16[32,48,768]{2,1,0:T(8,128)(2,1)}) %all-gather.18.cloned.1.call-update) | async-done | bytes 2359312 | tf_op jit(solution)/shard_map/all_gather | solution.py:289
  299.9 7.7 %fusion.7 = bf16[1536,768]{1,0:T(8,128)(2,1)S(1)} fusion(f32[1536,768]{1,0:T(8,128)} %copy-done.43, bf16[1536,768]{1,0:T(8,128)(2,1)} %bitcast.190, bf16[1,768,768]{2,1,0:T(8,128)(2,1)S(1)} %copy-done), kind=kOutput, calls=%fused_computation.9 | convolution fusion | flops 1835532288 | bytes 10616832 | tf_op jit(solution)/shard_map/dot_general | solution.py:32
  309.0 3.4 convolution_convert_fusion
  312.4 37.1 %reduce-scatter.6.cloned.1.call-done = bf16[384,768]{1,0:T(8,128)(2,1)} async-done(((bf16[1536,768]{1,0:T(8,128)(2,1)}), bf16[384,768]{1,0:T(8,128)(2,1)}) %reduce-scatter.6.cloned.1.call-update) | async-done | bytes 589840 | tf_op jit(solution)/shard_map/reduce_scatter | solution.py:295
  349.5 50.4 %reduce-scatter.8.cloned.1.call-done = bf16[384,768]{1,0:T(8,128)(2,1)} async-done(((bf16[1536,768]{1,0:T(8,128)(2,1)}), bf16[384,768]{1,0:T(8,128)(2,1)}) %reduce-scatter.8.cloned.1.call-update) | async-done | bytes 589840 | tf_op jit(solution)/shard_map/reduce_scatter | solution.py:300
  402.3 3.7 all-to-all-start.4
  407.2 15.5 %all-to-all-done.4 = bf16[8,96,768]{2,1,0:T(8,128)(2,1)S(1)} async-done(((bf16[8,96,768]{2,1,0:T(8,128)(2,1)}), bf16[8,96,768]{2,1,0:T(8,128)(2,1)S(1)}, u32[]{:S(2)}, u32[]{:S(2)}) %all-to-all-start.4) | async-done | bytes 1179680 | tf_op jit(solution)/shard_map/all_to_all | solution.py:167
  430.3 3.7 all-to-all-start.5
  434.0 5.4 convolution_convert_fusion.4
  442.2 4.4 all-to-all-start.8
  446.7 3.0 multiply_convert_fusion.1
  451.2 7.0 %convolution_bitcast_fusion = f32[1,768,768]{2,1,0:T(8,128)} fusion(bf16[1536,768]{1,0:T(8,128)(2,1)} %bitcast.191, f32[1536,768]{1,0:T(8,128)} %copy-done.43), kind=kOutput, calls=%fused_computation.22 | convolution fusion | flops 1822556160 | bytes 9437184 | tf_op jit(solution)/shard_map/dot_general | solution.py:32
  458.2 19.2 %shard_map.206 = (bf16[3,3,64,1024]{3,2,1,0:T(8,128)(2,1)S(1)}, f32[3,8,2048]{2,1,0:T(8,128)S(1)}) custom-call(bf16[3,3,64,1024]{3,2,1,0:T(8,128)(2,1)S(1)} %broadcast_multiply_fusion.qkv_ref, bf16[3,1024,1024]{2,1,0:T(8,128)(2,1)} %get-tuple-element.14.p_ref, bf16[8,3,64,128]{3,2,1,0:T(8,128)(2,1)S(1)} %bitcast.146), custom_call_target="tpu_custom_call" | custom-call | flops 1610612736 | bytes 6291456 | tf_op jit(solution)/shard_map/pallas_call | solution.py:131
  480.2 4.3 all-to-all-start.6
  489.2 3.8 reshape.275
  493.1 3.8 convolution_convert_fusion.5
  499.6 50.4 %reduce-scatter.12.cloned.1.call-done = bf16[24,768]{1,0:T(8,128)(2,1)} async-done(((bf16[768,768]{1,0:T(8,128)(2,1)}), bf16[24,768]{1,0:T(8,128)(2,1)}) %reduce-scatter.12.cloned.1.call-update) | async-done | bytes 36880 | tf_op jit(solution)/shard_map/reduce_scatter | solution.py:339
  553.4 41.6 %all-reduce.5 = f32[768,11]{0,1:T(8,128)S(1)} all-reduce(f32[768,11]{0,1:T(8,128)S(1)} %pad_maximum_fusion.2), channel_id=10, replica_groups=mesh['dp'=4,'ctx'=8] {'dp','ctx'}, use_global_device_ids=true, to_apply=%region_17.18.clone | all-reduce | flops 8448 | bytes 67584
  596.9 3.6 all-to-all-start.7
  601.6 5.5 all-to-all-done.7
  (236 shorter events, 72.0 us)
Async XLA Ops:
  7.2 248.4 %copy-start = (bf16[1,768,768]{2,1,0:T(8,128)(2,1)S(1)}, bf16[1,768,768]{2,1,0:T(8,128)(2,1)}, u32[]{:S(2)}) copy-start(bf16[1,768,768]{2,1,0:T(8,128)(2,1)} %param.21) | copy-start | bytes 3538948
  7.2 16.9 %copy-start.6 = (bf16[2,128,768]{2,1,0:T(8,128)(2,1)S(1)}, bf16[2,128,768]{2,1,0:T(8,128)(2,1)}, u32[]{:S(2)}) copy-start(bf16[2,128,768]{2,1,0:T(8,128)(2,1)} %param.14) | copy-start | bytes 1179652
  7.2 18.5 %copy-start.37 = (s32[2047]{0:T(1024)S(1)}, s32[2047]{0:T(1024)}, u32[]{:S(2)}) copy-start(s32[2047]{0:T(1024)} %param.24) | copy-start | bytes 24568
  7.2 45.5 %all-gather.12.cloned.1.call-start = ((), (), s32[]{:S(2)}) async-start(), calls=%async_computation.18 | async-start | bytes 1474560 | tf_op jit(solution)/shard_map/all_gather | solution.py:216
  22.7 65.6 %all-gather.14.cloned.1.call-start = ((), (), s32[]{:S(2)}) async-start(), calls=%async_computation.19 | async-start | bytes 3981312 | tf_op jit(solution)/shard_map/all_gather | solution.py:227
  24.9 120.5 %all-gather.10.cloned.1.call-start = ((), (), s32[]{:S(2)}) async-start(), calls=%async_computation.13 | async-start | bytes 1216512 | tf_op jit(solution)/shard_map/all_gather | solution.py:234
  25.8 64.0 %copy-start.38 = (s32[2048]{0:T(1024)}, s32[2048]{0:T(1024)S(1)}, u32[]{:S(2)}) copy-start(s32[2048]{0:T(1024)S(1)} %pad.23) | copy-start | bytes 24580
  98.2 23.7 %copy-start.40 = (s32[2,128]{1,0:T(2,128)S(1)}, s32[2,128]{1,0:T(2,128)}, u32[]{:S(2)}) copy-start(s32[2,128]{1,0:T(2,128)} %param.23) | copy-start | bytes 3076
  118.4 27.0 %all-to-all-start.1 = ((bf16[8,192,128]{2,1,0:T(8,128)(2,1)}), bf16[8,192,128]{2,1,0:T(8,128)(2,1)S(1)}, u32[]{:S(2)}, u32[]{:S(2)}) async-start(bf16[8,192,128]{2,1,0:T(8,128)(2,1)} %bitcast.12), calls=%async_computation.1 | async-start | bytes 786432 | tf_op jit(solution)/shard_map/all_to_all | solution.py:167
  121.9 127.4 %all-gather.16.cloned.1.call-start = ((), (), s32[]{:S(2)}) async-start(), calls=%async_computation.20 | async-start | bytes 2949120 | tf_op jit(solution)/shard_map/all_gather | solution.py:288
  148.2 277.3 %copy-start.5 = (f32[2,128,768]{2,1,0:T(8,128)}, f32[2,128,768]{2,1,0:T(8,128)S(1)}, u32[]{:S(2)}) copy-start(f32[2,128,768]{2,1,0:T(8,128)S(1)} %get-tuple-element.43) | copy-start | bytes 2359300
  175.8 124.1 %all-gather.18.cloned.1.call-start = ((), (), s32[]{:S(2)}) async-start(), calls=%async_computation.21 | async-start | bytes 2949120 | tf_op jit(solution)/shard_map/all_gather | solution.py:289
  176.4 173.1 %reduce-scatter.6.cloned.1.call-start = ((), (), s32[]{:S(2)}) async-start(), calls=%async_computation.14 | async-start | bytes 2949120 | tf_op jit(solution)/shard_map/reduce_scatter | solution.py:295
  259.9 140.0 %reduce-scatter.8.cloned.1.call-start = ((), (), s32[]{:S(2)}) async-start(), calls=%async_computation.15 | async-start | bytes 2949120 | tf_op jit(solution)/shard_map/reduce_scatter | solution.py:300
  299.9 9.1 %copy-start.13 = (bf16[4,192,768]{2,1,0:T(8,128)(2,1)S(1)}, bf16[4,192,768]{2,1,0:T(8,128)(2,1)}, u32[]{:S(2)}) copy-start(bf16[4,192,768]{2,1,0:T(8,128)(2,1)} %all_to_all.47) | copy-start | bytes 3538948
  402.3 20.5 %all-to-all-start.4 = ((bf16[8,96,768]{2,1,0:T(8,128)(2,1)}), bf16[8,96,768]{2,1,0:T(8,128)(2,1)S(1)}, u32[]{:S(2)}, u32[]{:S(2)}) async-start(bf16[8,96,768]{2,1,0:T(8,128)(2,1)} %pad_maximum_fusion.1), calls=%async_computation.6 | async-start | bytes 2359296 | tf_op jit(solution)/shard_map/all_to_all | solution.py:167
  407.2 15.8 %copy-start.12 = (bf16[2,128,768]{2,1,0:T(8,128)(2,1)S(1)}, bf16[2,128,768]{2,1,0:T(8,128)(2,1)}, u32[]{:S(2)}) copy-start(bf16[2,128,768]{2,1,0:T(8,128)(2,1)} %param.22) | copy-start | bytes 1179652
  428.8 20.8 %copy-start.3 = (f32[2,128,768]{2,1,0:T(8,128)}, f32[2,128,768]{2,1,0:T(8,128)S(1)}, u32[]{:S(2)}) copy-start(f32[2,128,768]{2,1,0:T(8,128)S(1)} %get-tuple-element.29) | copy-start | bytes 2359300
  430.3 11.9 %all-to-all-start.5 = ((bf16[8,192,128]{2,1,0:T(8,128)(2,1)}), bf16[8,192,128]{2,1,0:T(8,128)(2,1)S(1)}, u32[]{:S(2)}, u32[]{:S(2)}) async-start(bf16[8,192,128]{2,1,0:T(8,128)(2,1)} %bitcast.36), calls=%async_computation.7 | async-start | bytes 786432 | tf_op jit(solution)/shard_map/all_to_all | solution.py:167
  439.4 7.3 %copy-start.17 = (f32[8,128]{1,0:T(8,128)S(1)}, f32[8,128]{1,0:T(8,128)}, u32[]{:S(2)}) copy-start(f32[8,128]{1,0:T(8,128)} %get-tuple-element.38) | copy-start | bytes 12292
  442.2 7.5 %copy-start.11 = (bf16[8,192,128]{2,1,0:T(8,128)(2,1)S(1)}, bf16[8,192,128]{2,1,0:T(8,128)(2,1)}, u32[]{:S(2)}) copy-start(bf16[8,192,128]{2,1,0:T(8,128)(2,1)} %copy-done.10) | copy-start | bytes 1179652
  442.2 37.9 %all-to-all-start.8 = ((bf16[4,192,768]{2,1,0:T(8,128)(2,1)}), bf16[4,192,768]{2,1,0:T(8,128)(2,1)}, u32[]{:S(2)}, u32[]{:S(2)}) async-start(bf16[4,192,768]{2,1,0:T(8,128)(2,1)} %bitcast.164), calls=%async_computation.12 | async-start | bytes 2359296 | tf_op jit(solution)/shard_map/all_to_all | solution.py:167
  446.6 103.3 %reduce-scatter.12.cloned.1.call-start = ((), (), s32[]{:S(2)}) async-start(), calls=%async_computation.17 | async-start | bytes 1216512 | tf_op jit(solution)/shard_map/reduce_scatter | solution.py:339
  458.2 19.3 %copy-start.15 = (bf16[32,24,704]{2,1,0:T(8,128)(2,1)S(1)}, bf16[32,24,704]{2,1,0:T(8,128)(2,1)}, u32[]{:S(2)}) copy-start(bf16[32,24,704]{2,1,0:T(8,128)(2,1)} %all-gather.12.cloned.1.call-done) | copy-start | bytes 3244036
  480.2 71.2 %all-to-all-start.6 = ((bf16[8,128,768]{2,1,0:T(8,128)(2,1)}), bf16[8,128,768]{2,1,0:T(8,128)(2,1)}, u32[]{:S(2)}, u32[]{:S(2)}) async-start(bf16[8,128,768]{2,1,0:T(8,128)(2,1)} %bitcast.160), calls=%async_computation.8 | async-start | bytes 3145728 | tf_op jit(solution)/shard_map/all_to_all | solution.py:167
  484.5 112.4 %reduce-scatter.10.cloned.1.call-start = ((), (), s32[]{:S(2)}) async-start(), calls=%async_computation.16 | async-start | bytes 1228800 | tf_op jit(solution)/shard_map/reduce_scatter | solution.py:352
  497.0 56.1 %copy-start.7 = (bf16[2,128,768]{2,1,0:T(8,128)(2,1)S(1)}, bf16[2,128,768]{2,1,0:T(8,128)(2,1)}, u32[]{:S(2)}) copy-start(bf16[2,128,768]{2,1,0:T(8,128)(2,1)} %param.14) | copy-start | bytes 1179652
  497.0 56.1 %copy-start.32 = (f32[2,128]{1,0:T(2,128)S(1)}, f32[2,128]{1,0:T(2,128)}, u32[]{:S(2)}) copy-start(f32[2,128]{1,0:T(2,128)} %fusion.66) | copy-start | bytes 3076
  498.1 97.6 %copy-start.34 = (f32[2,128]{1,0:T(2,128)S(1)}, f32[2,128]{1,0:T(2,128)}, u32[]{:S(2)}) copy-start(f32[2,128]{1,0:T(2,128)} %copy-done.33) | copy-start | bytes 3076
  498.1 97.6 %copy-start.4 = (f32[2,128,768]{2,1,0:T(8,128)S(1)}, f32[2,128,768]{2,1,0:T(8,128)}, u32[]{:S(2)}) copy-start(f32[2,128,768]{2,1,0:T(8,128)} %copy-done.3) | copy-start | bytes 2359300
  595.7 13.2 %copy-start.1 = (bf16[1,768,768]{2,1,0:T(8,128)(2,1)S(1)}, bf16[1,768,768]{2,1,0:T(8,128)(2,1)}, u32[]{:S(2)}) copy-start(bf16[1,768,768]{2,1,0:T(8,128)(2,1)} %param.21) | copy-start | bytes 3538948
  596.9 10.3 %all-to-all-start.7 = ((bf16[8,24,576]{2,1,0:T(8,128)(2,1)}), bf16[8,24,576]{2,1,0:T(8,128)(2,1)S(1)}, u32[]{:S(2)}, u32[]{:S(2)}) async-start(bf16[8,24,576]{2,1,0:T(8,128)(2,1)} %bitcast.177), calls=%async_computation.10 | async-start | bytes 491520 | tf_op jit(solution)/shard_map/all_to_all | solution.py:167
  (27 other events, 51.6 us)
Sparse Core Ops, SparseCore 0:
  22.8 29.8 all-gather.11
  55.1 33.0 all-gather.13
  91.2 54.1 all-gather.9
  175.9 73.3 all-gather.15
  250.7 49.1 all-gather.17
  302.6 46.8 reduce-scatter.5
  352.4 47.5 reduce-scatter.7
  452.6 97.3 reduce-scatter.11
  552.3 25.6 reduce-scatter.9

commit v2 on v1

--- a/solution.py
+++ b/solution.py
@@ -231,7 +231,8 @@
     x_seq = spread[:, :block].reshape(length, width).astype(f32)
     seg_seq = spread[:, block, :block].reshape(length).astype(jnp.int32)
 
-    out_full = lax.all_gather(attn_out, ("dp", "ctx"), axis=0, tiled=True)
+    out_full = lax.all_gather(attn_out, "dp", axis=0, tiled=False)
+    out_full = lax.all_gather(out_full, "ctx", axis=1, tiled=False).reshape(width, width)
     win_part = swap(
         w_in[0].reshape(-1, dp_count, ff_part).transpose(1, 0, 2), "dp"
     ).reshape(width, ff_part)
@@ -248,6 +249,7 @@
     )
 
     normed_seq = rms_scale(x_seq, gain_first).astype(bf16)
+    normed_seq, win_part = lax.optimization_barrier((normed_seq, win_part))
     projected = dot(w_heads, normed_seq, 0, 1).astype(bf16).reshape(3, heads, DH, length)
     scale = jnp.array([DH**-0.5, 1.0, 1.0], bf16)[:, None, None, None]
     projected = projected * scale
@@ -336,9 +338,7 @@
     grad_mixed = jnp.pad(grad_mixed, ((0, 0), (0, all_cols - width), (0, 0)))
     grad_mixed = swap(grad_mixed.reshape(ctx_count, cols, block), "ctx")
     sum_out = jnp.einsum("bds,bse->de", mixed, grad_branch, preferred_element_type=f32)
-    grad_attn_out = lax.psum_scatter(
-        sum_out.astype(bf16), ("dp", "ctx"), scatter_dimension=0, tiled=True
-    ).astype(f32)
+    sum_out = lax.psum_scatter(sum_out.astype(bf16), "dp", scatter_dimension=0, tiled=True)
 
     grad_parts, diag = attend_back(
         projected, probs, grad_mixed.reshape(ctx_count, heads, DH, block)
@@ -352,6 +352,8 @@
     sum_qkv = lax.psum_scatter(
         dot(normed_seq, grad_parts, 0, 1).astype(bf16), "dp", scatter_dimension=0, tiled=True
     )
+    sum_out = swap(sum_out.reshape(ctx_count, own_rows, width), "ctx").astype(f32)
+    grad_attn_out = jnp.sum(sum_out, axis=0)
     sum_qkv = swap(sum_qkv.reshape(ctx_count, own_rows, 3 * cols), "ctx").astype(f32)
     sum_qkv = jnp.sum(sum_qkv.reshape(seqs, groups, own_rows, 3, cols), axis=0)
     grad_attn_qkv = sum_qkv.transpose(2, 1, 0, 3).reshape(3, own_rows, all_cols)[..., :width]
@@ -369,14 +371,11 @@
         jnp.zeros((NB, groups * heads), f32), sum_table, my_group * heads, axis=1
     )[:, :H]
     table_col = pad_last(sum_table.reshape(-1, table_rows), own_rows).reshape(width, 1)
-    sums = lax.psum_scatter(
-        jnp.concatenate(
-            [sum_gain_first[:, None], sum_gain_second[:, None], sum_router, table_col], axis=1
-        ),
-        ("dp", "ctx"),
-        scatter_dimension=0,
-        tiled=True,
-    )
+    sums = jnp.concatenate(
+        [sum_gain_first[:, None], sum_gain_second[:, None], sum_router, table_col], axis=1
+    )
+    sums = swap(sums.reshape(dp_count * ctx_count, own_rows, -1), ("dp", "ctx"))
+    sums = jnp.sum(sums, axis=0)
     return (
         output,
         grad_tokens,

time: 624 us -> 537 us (0.86)
  waiting for transfers between devices: 288 us -> 231 us
  blocking collectives: 136 us -> 103 us
  starting transfers between devices: 23.7 us -> 33 us
    all_gather x0 -> x1, blocking collectives: none -> 51 us  [on_device(): out_full = lax.all_gather(attn_out, 'dp', axis=0, tiled=False)]
    reduce_scatter x1, waiting for transfers between devices: 50.4 us -> 0.01 us  [on_device(): lax.psum_scatter(sum_out.astype(bf16), 'dp', scatter_dimension=0, tiled=T...]
    all_gather x1, waiting for transfers between devices: 5.12 us -> 48.9 us  [on_device(): rows_in = lax.all_gather(arrived[:, :slot_rows], 'dp', axis=0, tiled=False)]
    all_to_all x3, blocking collectives: 94.5 us -> 51.8 us  [swap(): return lax.all_to_all(values, axis, split_axis=0, concat_axis=0, tiled=True)]
    unnamed x1 -> x0, blocking collectives: 41.6 us -> none
    all_gather x1, waiting for transfers between devices: 26.8 us -> 0.01 us  [on_device(): layer = lax.all_gather(packed, 'dp', axis=0, tiled=False).reshape(width, -1)]
    all_gather x1, waiting for transfers between devices: 22.8 us -> 0.01 us  [on_device(): lax.all_gather(out_full, 'ctx', axis=1, tiled=False).reshape(width, width)]
    all_gather x1, waiting for transfers between devices: 30.6 us -> 19.7 us  [on_device(): lax.all_gather(jnp.concatenate([tokens, seg_rows], axis=1), 'ctx', axis=0...]
  transfers between devices with their start and end apart: 15 -> 17, of which waited for: 11 -> 11; matrix products, arithmetic and copies ran while one was open for 13% -> 15% of each run, Pallas kernels for 6% -> 7%
where the time goes in v2:
time: 537 us; the launch traced here: 529 us
  waiting for transfers between devices  231 us (43%)
  blocking collectives  103 us (19%)
  matrix products  54.9 us (10%)
  Pallas kernels  39.4 us (7%)
  starting transfers between devices  33 us (6%)
  local copies, waits for them, and re-layouts  31.9 us (6%)
  other arithmetic  20.6 us (4%)
  between operations  15.2 us (3%)
    all_to_all x3, blocking collectives, swap(): return lax.all_to_all(values, axis, split_axis=0, concat_axis=0, tiled=True)  51.8 us
    all_gather x1, blocking collectives, on_device(): out_full = lax.all_gather(attn_out, 'dp', axis=0, tiled=False)  51 us
    reduce_scatter x1, waiting for transfers between devices, on_device(): lax.psum_scatter(dot(grad_pre, win_part, 1, 1).astype(bf16), 'dp', scatte...  50.4 us
    all_gather x1, waiting for transfers between devices, on_device(): rows_in = lax.all_gather(arrived[:, :slot_rows], 'dp', axis=0, tiled=False)  48.9 us
    all_gather x1, waiting for transfers between devices, on_device(): grads_in = lax.all_gather(arrived[:, slot_rows:], 'dp', axis=0, tiled=False)  40.6 us
    dot_general x9, matrix products, dot(): lax.dot_general(a, b, (((ca,), (cb,)), ((), ())), preferred_element_type=...  40.6 us
    reduce_scatter x1, waiting for transfers between devices, on_device(): lax.psum_scatter(dot(expert_act, wout_part, 1, 0).astype(bf16), 'dp', sca...  37.1 us
    all_to_all x8, waiting for transfers between devices, swap(): return lax.all_to_all(values, axis, split_axis=0, concat_axis=0, tiled=True)  33.6 us
  transfers between devices with their start and end apart: 17, of which 11 were waited for; matrix products, arithmetic and copies ran while one was open for 15% of the time, Pallas kernels for 7%

profile of v2, /device:TPU:0, one launch (start us, length us, event | category | flops | bytes accessed | tf_op | source)
XLA Modules:
  0.0 528.8 jit_solution(13620264822625230717)
XLA Ops:
  10.3 12.4 %all_to_all.55 = bf16[8,24,704]{2,1,0:T(8,128)(2,1)} all-to-all(bf16[8,24,704]{2,1,0:T(8,128)(2,1)S(1)} %maximum_maximum_fusion), channel_id=1, replica_groups=mesh['dp'=4,'ctx'=8] {'ctx'}, dimensions={0} | all-to-all | bytes 540672 | tf_op jit(solution)/shard_map/all_to_all | solution.py:167
  28.8 4.9 all-to-all-start.1
  33.7 51.0 %all-gather.2 = bf16[96,768]{1,0:T(8,128)(2,1)} all-gather(bf16[24,768]{1,0:T(8,128)(2,1)S(1)} %copy-done.15), channel_id=4, replica_groups=mesh['dp'=4,'ctx'=8] {'dp'}, dimensions={0}, use_global_device_ids=true | all-gather | bytes 184320 | tf_op jit(solution)/shard_map/all_gather | solution.py:234
  90.0 19.7 %all-gather.14.cloned.1.call-done = bf16[16,144,768]{2,1,0:T(8,128)(2,1)} async-done(((bf16[2,144,768]{2,1,0:T(8,128)(2,1)}), bf16[16,144,768]{2,1,0:T(8,128)(2,1)}) %all-gather.14.cloned.1.call-update) | async-done | bytes 3538960 | tf_op jit(solution)/shard_map/all_gather | solution.py:227
  117.7 3.5 convolution_convert_fusion.3
  121.4 20.2 %shard_map.205 = (bf16[3,1024,1024]{2,1,0:T(8,128)(2,1)}, bf16[8,3,64,128]{3,2,1,0:T(8,128)(2,1)}) custom-call(bf16[3,3,64,1024]{3,2,1,0:T(8,128)(2,1)S(1)} %broadcast_multiply_fusion.qkv_ref, f32[3,8,2048]{2,1,0:T(8,128)S(1)} %stack.35.base_ref, s32[1024,1]{1,0:T(8,128)S(1)} %copy.108.segq_ref, s32[1,1024]{1,0:T(1,128)S(1)} %get-tuple-element.27.segk_ref), custom_call_target="tpu_custom_call" | custom-call | flops 805306368 | bytes 6291456 | tf_op jit(solution)/shard_map/pallas_call | solution.py:66
  141.6 4.1 all-to-all-start.2
  146.3 7.7 %all-to-all-done.2 = bf16[8,192,128]{2,1,0:T(8,128)(2,1)} async-done(((bf16[8,192,128]{2,1,0:T(8,128)(2,1)}), bf16[8,192,128]{2,1,0:T(8,128)(2,1)}, u32[]{:S(2)}, u32[]{:S(2)}) %all-to-all-start.2) | async-done | bytes 393248 | tf_op jit(solution)/shard_map/all_to_all | solution.py:167
  162.1 19.2 %all_to_all.56 = bf16[8,96,768]{2,1,0:T(8,128)(2,1)S(1)} all-to-all(bf16[8,96,768]{2,1,0:T(8,128)(2,1)S(1)} %pad_maximum_fusion), channel_id=1, replica_groups=mesh['dp'=4,'ctx'=8] {'ctx'}, dimensions={0} | all-to-all | bytes 2359296 | tf_op jit(solution)/shard_map/all_to_all | solution.py:167
  183.2 48.9 %all-gather.18.cloned.1.call-done = bf16[32,48,768]{2,1,0:T(8,128)(2,1)} async-done(((bf16[8,48,768]{2,1,0:T(8,128)(2,1)}), bf16[32,48,768]{2,1,0:T(8,128)(2,1)}) %all-gather.18.cloned.1.call-update) | async-done | bytes 2359312 | tf_op jit(solution)/shard_map/all_gather | solution.py:290
  232.2 4.0 fusion.73
  238.4 4.4 convolution_convert_fusion.1
  242.9 40.6 %all-gather.20.cloned.1.call-done = bf16[32,48,768]{2,1,0:T(8,128)(2,1)} async-done(((bf16[8,48,768]{2,1,0:T(8,128)(2,1)}), bf16[32,48,768]{2,1,0:T(8,128)(2,1)}) %all-gather.20.cloned.1.call-update) | async-done | bytes 2359312 | tf_op jit(solution)/shard_map/all_gather | solution.py:291
  283.5 7.6 %fusion.7 = bf16[1536,768]{1,0:T(8,128)(2,1)S(1)} fusion(f32[1536,768]{1,0:T(8,128)} %copy-done.39, bf16[1536,768]{1,0:T(8,128)(2,1)} %bitcast.197, bf16[1,768,768]{2,1,0:T(8,128)(2,1)S(1)} %copy-done), kind=kOutput, calls=%fused_computation.9 | convolution fusion | flops 1835532288 | bytes 10616832 | tf_op jit(solution)/shard_map/dot_general | solution.py:32
  292.5 3.4 convolution_convert_fusion
  296.0 37.1 %reduce-scatter.5.cloned.1.call-done = bf16[384,768]{1,0:T(8,128)(2,1)} async-done(((bf16[1536,768]{1,0:T(8,128)(2,1)}), bf16[384,768]{1,0:T(8,128)(2,1)}) %reduce-scatter.5.cloned.1.call-update) | async-done | bytes 589840 | tf_op jit(solution)/shard_map/reduce_scatter | solution.py:297
  333.1 50.4 %reduce-scatter.7.cloned.1.call-done = bf16[384,768]{1,0:T(8,128)(2,1)} async-done(((bf16[1536,768]{1,0:T(8,128)(2,1)}), bf16[384,768]{1,0:T(8,128)(2,1)}) %reduce-scatter.7.cloned.1.call-update) | async-done | bytes 589840 | tf_op jit(solution)/shard_map/reduce_scatter | solution.py:302
  384.9 20.2 %all_to_all.57 = bf16[8,96,768]{2,1,0:T(8,128)(2,1)S(1)} all-to-all(bf16[8,96,768]{2,1,0:T(8,128)(2,1)S(1)} %pad_maximum_fusion.1), channel_id=1, replica_groups=mesh['dp'=4,'ctx'=8] {'ctx'}, dimensions={0} | all-to-all | bytes 2359296 | tf_op jit(solution)/shard_map/all_to_all | solution.py:167
  411.9 3.7 all-to-all-start.5
  415.5 5.4 %convolution_convert_fusion.4 = bf16[768,768]{1,0:T(8,128)(2,1)} fusion(bf16[1536,768]{1,0:T(8,128)(2,1)} %bitcast.200, bf16[1536,768]{1,0:T(8,128)(2,1)} %copy-done.38), kind=kOutput, calls=%fused_computation.30 | convolution fusion | flops 1812529152 | bytes 5898240 | tf_op jit(solution)/shard_map/dot_general | solution.py:32
  423.8 4.3 all-to-all-start.10
  428.1 19.3 %shard_map.206 = (bf16[3,3,64,1024]{3,2,1,0:T(8,128)(2,1)S(1)}, f32[3,8,2048]{2,1,0:T(8,128)S(1)}) custom-call(bf16[3,3,64,1024]{3,2,1,0:T(8,128)(2,1)S(1)} %broadcast_multiply_fusion.qkv_ref, bf16[3,1024,1024]{2,1,0:T(8,128)(2,1)} %get-tuple-element.18.p_ref, bf16[8,3,64,128]{3,2,1,0:T(8,128)(2,1)S(1)} %bitcast.152), custom_call_target="tpu_custom_call" | custom-call | flops 1610612736 | bytes 6291456 | tf_op jit(solution)/shard_map/pallas_call | solution.py:131
  450.0 7.1 %convolution_bitcast_fusion = f32[1,768,768]{2,1,0:T(8,128)} fusion(bf16[1536,768]{1,0:T(8,128)(2,1)} %bitcast.198, f32[1536,768]{1,0:T(8,128)} %copy-done.39), kind=kOutput, calls=%fused_computation.21 | convolution fusion | flops 1822556160 | bytes 9437184 | tf_op jit(solution)/shard_map/dot_general | solution.py:32
  459.8 4.4 all-to-all-start.6
  471.5 3.8 reshape.277
  478.1 7.2 %all-to-all-done.6 = bf16[8,128,768]{2,1,0:T(8,128)(2,1)} async-done(((bf16[8,128,768]{2,1,0:T(8,128)(2,1)}), bf16[8,128,768]{2,1,0:T(8,128)(2,1)}, u32[]{:S(2)}, u32[]{:S(2)}) %all-to-all-start.6) | async-done | bytes 1572896 | tf_op jit(solution)/shard_map/all_to_all | solution.py:167
  488.3 4.1 all-to-all-start.9
  492.4 8.0 %all-to-all-done.9 = f32[32,1,264]{2,1,0:T(1,128)S(1)} async-done(((f32[32,1,264]{2,1,0:T(1,128)}), f32[32,1,264]{2,1,0:T(1,128)S(1)}, u32[]{:S(2)}, u32[]{:S(2)}) %all-to-all-start.9) | async-done | bytes 33824 | tf_op jit(solution)/shard_map/all_to_all | solution.py:167
  500.4 3.4 all-to-all-start.7
  506.4 4.1 all-to-all-done.7
  510.5 3.4 all-to-all-start.8
  517.4 3.7 all-to-all-done.8
  (237 shorter events, 72.3 us)
Async XLA Ops:
  7.2 231.2 %copy-start = (bf16[1,768,768]{2,1,0:T(8,128)(2,1)S(1)}, bf16[1,768,768]{2,1,0:T(8,128)(2,1)}, u32[]{:S(2)}) copy-start(bf16[1,768,768]{2,1,0:T(8,128)(2,1)} %param.21) | copy-start | bytes 3538948
  7.2 16.9 %copy-start.5 = (bf16[2,128,768]{2,1,0:T(8,128)(2,1)S(1)}, bf16[2,128,768]{2,1,0:T(8,128)(2,1)}, u32[]{:S(2)}) copy-start(bf16[2,128,768]{2,1,0:T(8,128)(2,1)} %param.14) | copy-start | bytes 1179652
  7.2 77.7 %all-gather.12.cloned.1.call-start = ((), (), s32[]{:S(2)}) async-start(), calls=%async_computation.19 | async-start | bytes 1474560 | tf_op jit(solution)/shard_map/all_gather | solution.py:216
  22.7 86.9 %all-gather.14.cloned.1.call-start = ((), (), s32[]{:S(2)}) async-start(), calls=%async_computation.20 | async-start | bytes 3981312 | tf_op jit(solution)/shard_map/all_gather | solution.py:227
  27.6 6.0 %copy-start.15 = (bf16[24,768]{1,0:T(8,128)(2,1)S(1)}, bf16[24,768]{1,0:T(8,128)(2,1)}, u32[]{:S(2)}) copy-start(bf16[24,768]{1,0:T(8,128)(2,1)} %param.16) | copy-start | bytes 110596
  27.6 57.0 %copy-start.33 = (s32[2047]{0:T(1024)S(1)}, s32[2047]{0:T(1024)}, u32[]{:S(2)}) copy-start(s32[2047]{0:T(1024)} %param.24) | copy-start | bytes 24568
  28.8 88.9 %all-to-all-start.1 = ((bf16[4,192,768]{2,1,0:T(8,128)(2,1)}), bf16[4,192,768]{2,1,0:T(8,128)(2,1)S(1)}, u32[]{:S(2)}, u32[]{:S(2)}) async-start(bf16[4,192,768]{2,1,0:T(8,128)(2,1)} %copy.107), calls=%async_computation.1 | async-start | bytes 2359296 | tf_op jit(solution)/shard_map/all_to_all | solution.py:167
  33.7 112.7 %all-gather.16.cloned.1.call-start = ((), (), s32[]{:S(2)}) async-start(), calls=%async_computation.21 | async-start | bytes 1327104 | tf_op jit(solution)/shard_map/all_gather | solution.py:235
  121.4 24.3 %copy-start.36 = (s32[2,128]{1,0:T(2,128)S(1)}, s32[2,128]{1,0:T(2,128)}, u32[]{:S(2)}) copy-start(s32[2,128]{1,0:T(2,128)} %param.23) | copy-start | bytes 3076
  141.6 12.5 %all-to-all-start.2 = ((bf16[8,192,128]{2,1,0:T(8,128)(2,1)}), bf16[8,192,128]{2,1,0:T(8,128)(2,1)}, u32[]{:S(2)}, u32[]{:S(2)}) async-start(bf16[8,192,128]{2,1,0:T(8,128)(2,1)} %bitcast.14), calls=%async_computation.2 | async-start | bytes 786432 | tf_op jit(solution)/shard_map/all_to_all | solution.py:167
  145.7 86.4 %all-gather.18.cloned.1.call-start = ((), (), s32[]{:S(2)}) async-start(), calls=%async_computation.22 | async-start | bytes 2949120 | tf_op jit(solution)/shard_map/all_gather | solution.py:290
  156.8 5.2 copy-start.7
  182.4 101.1 %all-gather.20.cloned.1.call-start = ((), (), s32[]{:S(2)}) async-start(), calls=%async_computation.23 | async-start | bytes 2949120 | tf_op jit(solution)/shard_map/all_gather | solution.py:291
  183.0 150.1 %reduce-scatter.5.cloned.1.call-start = ((), (), s32[]{:S(2)}) async-start(), calls=%async_computation.15 | async-start | bytes 2949120 | tf_op jit(solution)/shard_map/reduce_scatter | solution.py:297
  242.8 140.7 %reduce-scatter.7.cloned.1.call-start = ((), (), s32[]{:S(2)}) async-start(), calls=%async_computation.16 | async-start | bytes 2949120 | tf_op jit(solution)/shard_map/reduce_scatter | solution.py:302
  283.5 9.1 %copy-start.13 = (bf16[4,192,768]{2,1,0:T(8,128)(2,1)S(1)}, bf16[4,192,768]{2,1,0:T(8,128)(2,1)}, u32[]{:S(2)}) copy-start(bf16[4,192,768]{2,1,0:T(8,128)(2,1)} %copy-done.12) | copy-start | bytes 3538948
  411.9 11.9 %all-to-all-start.5 = ((bf16[8,192,128]{2,1,0:T(8,128)(2,1)}), bf16[8,192,128]{2,1,0:T(8,128)(2,1)S(1)}, u32[]{:S(2)}, u32[]{:S(2)}) async-start(bf16[8,192,128]{2,1,0:T(8,128)(2,1)} %bitcast.39), calls=%async_computation.7 | async-start | bytes 786432 | tf_op jit(solution)/shard_map/all_to_all | solution.py:167
  423.8 36.0 %all-to-all-start.10 = ((bf16[4,192,768]{2,1,0:T(8,128)(2,1)}), bf16[4,192,768]{2,1,0:T(8,128)(2,1)}, u32[]{:S(2)}, u32[]{:S(2)}) async-start(bf16[4,192,768]{2,1,0:T(8,128)(2,1)} %bitcast.59), calls=%async_computation.14 | async-start | bytes 2359296 | tf_op jit(solution)/shard_map/all_to_all | solution.py:167
  428.1 72.3 %reduce-scatter.9.cloned.1.call-start = ((), (), s32[]{:S(2)}) async-start(), calls=%async_computation.17 | async-start | bytes 1228800 | tf_op jit(solution)/shard_map/reduce_scatter | solution.py:352
  428.1 19.3 %copy-start.11 = (bf16[1024,768]{1,0:T(8,128)(2,1)S(1)}, bf16[1024,768]{1,0:T(8,128)(2,1)}, u32[]{:S(2)}) copy-start(bf16[1024,768]{1,0:T(8,128)(2,1)} %fusion.9) | copy-start | bytes 4718596
  450.0 7.1 %copy-start.14 = (bf16[32,24,704]{2,1,0:T(8,128)(2,1)S(1)}, bf16[32,24,704]{2,1,0:T(8,128)(2,1)}, u32[]{:S(2)}) copy-start(bf16[32,24,704]{2,1,0:T(8,128)(2,1)} %all-gather.12.cloned.1.call-done) | copy-start | bytes 3244036
  459.8 4.8 copy-start.4
  459.8 25.5 %all-to-all-start.6 = ((bf16[8,128,768]{2,1,0:T(8,128)(2,1)}), bf16[8,128,768]{2,1,0:T(8,128)(2,1)}, u32[]{:S(2)}, u32[]{:S(2)}) async-start(bf16[8,128,768]{2,1,0:T(8,128)(2,1)} %bitcast.166), calls=%async_computation.8 | async-start | bytes 3145728 | tf_op jit(solution)/shard_map/all_to_all | solution.py:167
  464.2 46.3 %reduce-scatter.11.cloned.1.call-start = ((), (), s32[]{:S(2)}) async-start(), calls=%async_computation.18 | async-start | bytes 1474560 | tf_op jit(solution)/shard_map/reduce_scatter | solution.py:341
  471.5 3.9 copy-start.23
  471.5 3.9 copy-start.32
  471.5 4.3 copy-start.17
  471.5 5.2 copy-start.35
  488.3 12.1 %all-to-all-start.9 = ((f32[32,1,264]{2,1,0:T(1,128)}), f32[32,1,264]{2,1,0:T(1,128)S(1)}, u32[]{:S(2)}, u32[]{:S(2)}) async-start(f32[32,1,264]{2,1,0:T(1,128)} %reshape.295), calls=%async_computation.13 | async-start | bytes 98304 | tf_op jit(solution)/shard_map/all_to_all | solution.py:167
  500.4 10.1 %all-to-all-start.7 = ((bf16[8,24,576]{2,1,0:T(8,128)(2,1)}), bf16[8,24,576]{2,1,0:T(8,128)(2,1)S(1)}, u32[]{:S(2)}, u32[]{:S(2)}) async-start(bf16[8,24,576]{2,1,0:T(8,128)(2,1)} %bitcast.184), calls=%async_computation.10 | async-start | bytes 491520 | tf_op jit(solution)/shard_map/all_to_all | solution.py:167
  506.2 15.6 %copy-start.1 = (bf16[1,768,768]{2,1,0:T(8,128)(2,1)S(1)}, bf16[1,768,768]{2,1,0:T(8,128)(2,1)}, u32[]{:S(2)}) copy-start(bf16[1,768,768]{2,1,0:T(8,128)(2,1)} %param.21) | copy-start | bytes 3538948
  510.5 10.6 %all-to-all-start.8 = ((bf16[8,24,768]{2,1,0:T(8,128)(2,1)}), bf16[8,24,768]{2,1,0:T(8,128)(2,1)S(1)}, u32[]{:S(2)}, u32[]{:S(2)}) async-start(bf16[8,24,768]{2,1,0:T(8,128)(2,1)} %bitcast.183), calls=%async_computation.12 | async-start | bytes 589824 | tf_op jit(solution)/shard_map/all_to_all | solution.py:167
  (25 other events, 54.1 us)
Sparse Core Ops, SparseCore 0:
  22.8 50.6 all-gather.11
  76.0 33.6 all-gather.13
  111.6 24.1 all-gather.15
  182.5 49.5 all-gather.17
  234.1 49.2 all-gather.19
  286.2 46.8 reduce-scatter.4
  336.0 47.5 reduce-scatter.6
  450.0 25.5 reduce-scatter.8
  478.0 28.5 reduce-scatter.10
